TPU v7x, 32 devices: a whole 2x2x4 slice. The times are simulated.
32 devices in a mesh: tm: 2 (over core), sx: 4 (over y, x), sy: 4 (over z).
Axes of the slice: x: 2, y: 2, z: 4, core: 2. Of those that a mesh axis runs over, the one named last changes fastest.
Arguments:
- slices_state: float32 [2, 64, 16, 16, 128], P('tm', None, 'sx', 'sy'), may hold values from -6 to 6
- forcing: float32 [2, 64, 16, 16, 128], P('tm', None, 'sx', 'sy'), may hold values from -0.6 to 0.6
- initial: float32 [64, 16, 16, 128], P(None, 'sx', 'sy'), may hold values from -6 to 6
- volume: float32 [64, 64], replicated, may hold values from -0.06 to 0.06
- lift: float32 [6, 64, 16], replicated, may hold values from -0.024 to 0.024
Outputs:
- corrected: float32 [2, 64, 16, 16, 128], P('tm', None, 'sx', 'sy')
- residual: float32 [2, 64, 16, 16, 128], P('tm', None, 'sx', 'sy')
All inputs are finite; a program needn't handle non-finite values.
Results may differ from a plain program's by a relative error of at most 0.00018.
Values sent between devices are 32-bit elements; how exact they have to be, the bound alone decides.
A program may use at most 64 MiB of HBM per device.

v0:
```python
import jax
import jax.numpy as jnp
from jax import lax
from jax.sharding import PartitionSpec as P


def padded_2(array, sides, width):
    for axis, dim in sides:
        size, length = (lax.axis_size(axis), array.shape[dim])
        up = [(i, (i + 1) % size) for i in range(size - 1)]
        down = [(j, i) for i, j in up]
        last = lax.slice_in_dim(array, length - width, length, axis=dim)
        initial = lax.slice_in_dim(array, 0, width, axis=dim)
        before = lax.ppermute(last, axis, up)
        after = lax.ppermute(initial, axis, down)
        array = jnp.concatenate([before, array, after], axis=dim)
    return array


def passed_along(value, axis, steps):
    count = lax.axis_size(axis)
    initial, last = (max(0, -steps), min(count, count - steps))
    return lax.ppermute(value, axis, [(source, source + steps) for source in range(initial, last)])


def lower_side(t, axis):
    count = t.shape[axis]
    zero = jnp.zeros_like(lax.slice_in_dim(t, 0, 1, axis=axis))
    return jnp.concatenate([zero, lax.slice_in_dim(t, 0, count - 1, axis=axis)], axis)


def upper_side(t, axis):
    count = t.shape[axis]
    zero = jnp.zeros_like(lax.slice_in_dim(t, 0, 1, axis=axis))
    return jnp.concatenate([lax.slice_in_dim(t, 1, count, axis=axis), zero], axis)


def planes(cube, shape):
    x_plus = cube[3].reshape((16,) + shape)
    x_minus = cube[0].reshape((16,) + shape)
    y_plus = cube[:, 3].reshape((16,) + shape)
    y_minus = cube[:, 0].reshape((16,) + shape)
    return (x_plus, x_minus, y_plus, y_minus)


def delta(field, weight, lift_flat):
    width, nx, ny, nz = field.shape
    cube = field.reshape(4, 4, 4, nx, ny, nz)
    z_plus = cube[:, :, 3].reshape(16, nx, ny, nz)
    z_minus = cube[:, :, 0].reshape(16, nx, ny, nz)
    padded = padded_2(field, (("sx", 1), ("sy", 2)), 1)
    wide = padded.reshape(4, 4, 4, nx + 2, ny + 2, nz)
    x_plus, x_minus, y_plus, y_minus = planes(wide, (nx + 2, ny + 2, nz))
    below_x = x_plus[:, :nx, 1 : ny + 1]
    above_x = x_minus[:, 2:, 1 : ny + 1]
    below_y = y_plus[:, 1 : nx + 1, :ny]
    above_y = y_minus[:, 1 : nx + 1, 2:]
    stacked = jnp.concatenate(
        [below_x, above_x, below_y, above_y, lower_side(z_plus, 3), upper_side(z_minus, 3)], 0
    ).reshape(96, -1)
    own = jnp.dot(
        weight,
        field.reshape(width, -1),
        precision=lax.Precision.HIGHEST,
        preferred_element_type=jnp.float32,
    )
    faces = jnp.dot(
        lift_flat, stacked, precision=lax.Precision.HIGHEST, preferred_element_type=jnp.float32
    )
    return (own + faces).reshape(field.shape)


def local(slices_state, forcing, initial, volume, lift):
    weight = volume - 0.1 * jnp.eye(volume.shape[0], dtype=jnp.float32)
    lift_flat = jnp.transpose(lift, (1, 0, 2)).reshape(volume.shape[0], 96)
    state = slices_state[0]
    source = forcing[0]
    received = passed_along(slices_state, "tm", 1)[0]
    start = jnp.where(lax.axis_index("tm") == 0, initial, received)
    relaxed = start
    for step in range(3):
        relaxed = relaxed + delta(relaxed, weight, lift_flat) + source
    resid = relaxed + delta(relaxed, weight, lift_flat) + source - state

    def coarse(field):
        return field + 4.0 * delta(field, weight, lift_flat)

    count = lax.axis_size("tm")

    def advance(turn, error_now):
        before = passed_along(error_now, "tm", 1)
        return coarse(before) + resid

    error = lax.fori_loop(0, count - 1, advance, resid)
    corrected = state + error
    return (corrected[None], resid[None])


def solution(mesh):
    placed = (
        P("tm", None, "sx", "sy", None),
        P("tm", None, "sx", "sy", None),
        P(None, "sx", "sy", None),
        P(),
        P(),
    )
    return jax.shard_map(
        local,
        mesh=mesh,
        in_specs=placed,
        out_specs=(P("tm", None, "sx", "sy", None), P("tm", None, "sx", "sy", None)),
        check_vma=False,
    )
```

profile of v0, /device:TPU:0, one launch (start us, length us, event | category | flops | bytes accessed | tf_op | source)
XLA Modules:
  0.0 139.3 jit_solution(12547819180031769431)
XLA Ops:
  0.6 2.5 %collective-permute-start = (f32[1,64,4,4,128]{4,3,2,1,0:T(4,128)}, f32[1,64,4,4,128]{4,3,2,1,0:T(4,128)S(1)}, u32[]{:S(2)}, u32[]{:S(2)}) collective-permute-start(f32[1,64,4,4,128]{4,3,2,1,0:T(4,128)} %param.5), channel_id=1, source_target_pairs={{0,16},{1,17},{2,18},{3,19},{4,20},{5,21},{6,22},{7,23},{8,24},{9,... | collective-permute-start | bytes 1572872 | tf_op jit(solution)/shard_map/ppermute | solution.py:23
  3.2 1.7 %collective-permute-done = f32[1,64,4,4,128]{4,3,2,1,0:T(4,128)S(1)} collective-permute-done((f32[1,64,4,4,128]{4,3,2,1,0:T(4,128)}, f32[1,64,4,4,128]{4,3,2,1,0:T(4,128)S(1)}, u32[]{:S(2)}, u32[]{:S(2)}) %collective-permute-start) | collective-permute-done | bytes 524320 | tf_op jit(solution)/shard_map/ppermute | solution.py:23
  6.3 4.2 %collective-permute-start.1 = (f32[64,1,4,128]{3,2,1,0:T(4,128)S(1)}, f32[64,1,4,128]{3,2,1,0:T(4,128)S(1)}, u32[]{:S(2)}, u32[]{:S(2)}) collective-permute-start(f32[64,1,4,128]{3,2,1,0:T(4,128)S(1)} %get-tuple-element.56), channel_id=1, source_target_pairs={{0,4},{4,8},{8,12},{1,5},{5,9},{9,13},{2,6},{6,10},{10,14},{3,7},{... | collective-permute-start | bytes 393224 | tf_op jit(solution)/shard_map/ppermute | solution.py:14
  13.1 4.7 %collective-permute-done.2 = f32[64,1,4,128]{3,2,1,0:T(4,128)S(1)} collective-permute-done((f32[64,1,4,128]{3,2,1,0:T(4,128)S(1)}, f32[64,1,4,128]{3,2,1,0:T(4,128)S(1)}, u32[]{:S(2)}, u32[]{:S(2)}) %collective-permute-start.2) | collective-permute-done | bytes 131104 | tf_op jit(solution)/shard_map/ppermute | solution.py:15
  18.1 3.5 %collective-permute-start.3 = (f32[64,6,1,128]{3,2,1,0:T(1,128)S(1)}, f32[64,6,1,128]{3,2,1,0:T(1,128)S(1)}, u32[]{:S(2)}, u32[]{:S(2)}) collective-permute-start(f32[64,6,1,128]{3,2,1,0:T(1,128)S(1)} %get-tuple-element.35), channel_id=1, source_target_pairs={{0,1},{1,2},{2,3},{4,5},{5,6},{6,7},{8,9},{9,10},{10,11},{12,13},{... | collective-permute-start | bytes 589832 | tf_op jit(solution)/shard_map/ppermute | solution.py:14
  23.0 1.9 %collective-permute-done.3 = f32[64,6,1,128]{3,2,1,0:T(1,128)S(1)} collective-permute-done((f32[64,6,1,128]{3,2,1,0:T(1,128)S(1)}, f32[64,6,1,128]{3,2,1,0:T(1,128)S(1)}, u32[]{:S(2)}, u32[]{:S(2)}) %collective-permute-start.3) | collective-permute-done | bytes 196640 | tf_op jit(solution)/shard_map/ppermute | solution.py:14
  24.9 4.3 %collective-permute-done.4 = f32[64,6,1,128]{3,2,1,0:T(1,128)S(1)} collective-permute-done((f32[64,6,1,128]{3,2,1,0:T(1,128)S(1)}, f32[64,6,1,128]{3,2,1,0:T(1,128)S(1)}, u32[]{:S(2)}, u32[]{:S(2)}) %collective-permute-start.4) | collective-permute-done | bytes 196640 | tf_op jit(solution)/shard_map/ppermute | solution.py:15
  32.6 3.9 %collective-permute-start.5 = (f32[64,1,4,128]{3,2,1,0:T(4,128)S(1)}, f32[64,1,4,128]{3,2,1,0:T(4,128)S(1)}, u32[]{:S(2)}, u32[]{:S(2)}) collective-permute-start(f32[64,1,4,128]{3,2,1,0:T(4,128)S(1)} %get-tuple-element.52), channel_id=1, source_target_pairs={{0,4},{4,8},{8,12},{1,5},{5,9},{9,13},{2,6},{6,10},{10,14},{3,7},{... | collective-permute-start | bytes 393224 | tf_op jit(solution)/shard_map/ppermute | solution.py:14
  39.1 4.4 %collective-permute-done.6 = f32[64,1,4,128]{3,2,1,0:T(4,128)S(1)} collective-permute-done((f32[64,1,4,128]{3,2,1,0:T(4,128)S(1)}, f32[64,1,4,128]{3,2,1,0:T(4,128)S(1)}, u32[]{:S(2)}, u32[]{:S(2)}) %collective-permute-start.6) | collective-permute-done | bytes 131104 | tf_op jit(solution)/shard_map/ppermute | solution.py:15
  43.7 3.5 %collective-permute-start.7 = (f32[64,6,1,128]{3,2,1,0:T(1,128)S(1)}, f32[64,6,1,128]{3,2,1,0:T(1,128)S(1)}, u32[]{:S(2)}, u32[]{:S(2)}) collective-permute-start(f32[64,6,1,128]{3,2,1,0:T(1,128)S(1)} %get-tuple-element.33), channel_id=1, source_target_pairs={{0,1},{1,2},{2,3},{4,5},{5,6},{6,7},{8,9},{9,10},{10,11},{12,13},{... | collective-permute-start | bytes 589832 | tf_op jit(solution)/shard_map/ppermute | solution.py:14
  48.6 1.8 %collective-permute-done.7 = f32[64,6,1,128]{3,2,1,0:T(1,128)S(1)} collective-permute-done((f32[64,6,1,128]{3,2,1,0:T(1,128)S(1)}, f32[64,6,1,128]{3,2,1,0:T(1,128)S(1)}, u32[]{:S(2)}, u32[]{:S(2)}) %collective-permute-start.7) | collective-permute-done | bytes 196640 | tf_op jit(solution)/shard_map/ppermute | solution.py:14
  50.4 4.4 %collective-permute-done.8 = f32[64,6,1,128]{3,2,1,0:T(1,128)S(1)} collective-permute-done((f32[64,6,1,128]{3,2,1,0:T(1,128)S(1)}, f32[64,6,1,128]{3,2,1,0:T(1,128)S(1)}, u32[]{:S(2)}, u32[]{:S(2)}) %collective-permute-start.8) | collective-permute-done | bytes 196640 | tf_op jit(solution)/shard_map/ppermute | solution.py:15
  59.4 4.6 %collective-permute-start.9 = (f32[64,1,4,128]{3,2,1,0:T(4,128)S(1)}, f32[64,1,4,128]{3,2,1,0:T(4,128)S(1)}, u32[]{:S(2)}, u32[]{:S(2)}) collective-permute-start(f32[64,1,4,128]{3,2,1,0:T(4,128)S(1)} %get-tuple-element.48), channel_id=1, source_target_pairs={{0,4},{4,8},{8,12},{1,5},{5,9},{9,13},{2,6},{6,10},{10,14},{3,7},{... | collective-permute-start | bytes 393224 | tf_op jit(solution)/shard_map/ppermute | solution.py:14
  66.8 3.5 %collective-permute-start.11 = (f32[64,6,1,128]{3,2,1,0:T(1,128)S(1)}, f32[64,6,1,128]{3,2,1,0:T(1,128)S(1)}, u32[]{:S(2)}, u32[]{:S(2)}) collective-permute-start(f32[64,6,1,128]{3,2,1,0:T(1,128)S(1)} %get-tuple-element.31), channel_id=1, source_target_pairs={{0,1},{1,2},{2,3},{4,5},{5,6},{6,7},{8,9},{9,10},{10,11},{12,13},{... | collective-permute-start | bytes 589832 | tf_op jit(solution)/shard_map/ppermute | solution.py:14
  73.4 4.4 %collective-permute-done.12 = f32[64,6,1,128]{3,2,1,0:T(1,128)S(1)} collective-permute-done((f32[64,6,1,128]{3,2,1,0:T(1,128)S(1)}, f32[64,6,1,128]{3,2,1,0:T(1,128)S(1)}, u32[]{:S(2)}, u32[]{:S(2)}) %collective-permute-start.12) | collective-permute-done | bytes 196640 | tf_op jit(solution)/shard_map/ppermute | solution.py:15
  81.2 4.4 %collective-permute-start.13 = (f32[64,1,4,128]{3,2,1,0:T(4,128)S(1)}, f32[64,1,4,128]{3,2,1,0:T(4,128)S(1)}, u32[]{:S(2)}, u32[]{:S(2)}) collective-permute-start(f32[64,1,4,128]{3,2,1,0:T(4,128)S(1)} %get-tuple-element.44), channel_id=1, source_target_pairs={{0,4},{4,8},{8,12},{1,5},{5,9},{9,13},{2,6},{6,10},{10,14},{3,7},{... | collective-permute-start | bytes 393224 | tf_op jit(solution)/shard_map/ppermute | solution.py:14
  88.1 5.6 %collective-permute-done.14 = f32[64,1,4,128]{3,2,1,0:T(4,128)S(1)} collective-permute-done((f32[64,1,4,128]{3,2,1,0:T(4,128)S(1)}, f32[64,1,4,128]{3,2,1,0:T(4,128)S(1)}, u32[]{:S(2)}, u32[]{:S(2)}) %collective-permute-start.14) | collective-permute-done | bytes 131104 | tf_op jit(solution)/shard_map/ppermute | solution.py:15
  94.0 1.9 %collective-permute-start.15 = (f32[64,6,1,128]{3,2,1,0:T(1,128)S(1)}, f32[64,6,1,128]{3,2,1,0:T(1,128)S(1)}, u32[]{:S(2)}, u32[]{:S(2)}) collective-permute-start(f32[64,6,1,128]{3,2,1,0:T(1,128)S(1)} %get-tuple-element.29), channel_id=1, source_target_pairs={{0,1},{1,2},{2,3},{4,5},{5,6},{6,7},{8,9},{9,10},{10,11},{12,13},{... | collective-permute-start | bytes 589832 | tf_op jit(solution)/shard_map/ppermute | solution.py:14
  97.3 1.8 %collective-permute-done.15 = f32[64,6,1,128]{3,2,1,0:T(1,128)S(1)} collective-permute-done((f32[64,6,1,128]{3,2,1,0:T(1,128)S(1)}, f32[64,6,1,128]{3,2,1,0:T(1,128)S(1)}, u32[]{:S(2)}, u32[]{:S(2)}) %collective-permute-start.15) | collective-permute-done | bytes 196640 | tf_op jit(solution)/shard_map/ppermute | solution.py:14
  99.1 4.4 %collective-permute-done.16 = f32[64,6,1,128]{3,2,1,0:T(1,128)S(1)} collective-permute-done((f32[64,6,1,128]{3,2,1,0:T(1,128)S(1)}, f32[64,6,1,128]{3,2,1,0:T(1,128)S(1)}, u32[]{:S(2)}, u32[]{:S(2)}) %collective-permute-start.16) | collective-permute-done | bytes 196640 | tf_op jit(solution)/shard_map/ppermute | solution.py:15
  109.6 4.8 %collective-permute-start.18 = (f32[64,1,4,128]{3,2,1,0:T(4,128)S(1)}, f32[64,1,4,128]{3,2,1,0:T(4,128)S(1)}, u32[]{:S(2)}, u32[]{:S(2)}) collective-permute-start(f32[64,1,4,128]{3,2,1,0:T(4,128)S(1)} %get-tuple-element.40), channel_id=1, source_target_pairs={{0,4},{4,8},{8,12},{1,5},{5,9},{9,13},{2,6},{6,10},{10,14},{3,7},{... | collective-permute-start | bytes 393224 | tf_op jit(solution)/shard_map/while/body/eval_jaxpr/ppermute | solution.py:14
  117.8 4.0 %collective-permute-done.19 = f32[64,1,4,128]{3,2,1,0:T(4,128)S(1)} collective-permute-done((f32[64,1,4,128]{3,2,1,0:T(4,128)S(1)}, f32[64,1,4,128]{3,2,1,0:T(4,128)S(1)}, u32[]{:S(2)}, u32[]{:S(2)}) %collective-permute-start.19) | collective-permute-done | bytes 131104 | tf_op jit(solution)/shard_map/while/body/eval_jaxpr/ppermute | solution.py:15
  122.2 1.9 %collective-permute-start.20 = (f32[64,6,1,128]{3,2,1,0:T(1,128)S(1)}, f32[64,6,1,128]{3,2,1,0:T(1,128)S(1)}, u32[]{:S(2)}, u32[]{:S(2)}) collective-permute-start(f32[64,6,1,128]{3,2,1,0:T(1,128)S(1)} %get-tuple-element.27), channel_id=1, source_target_pairs={{0,1},{1,2},{2,3},{4,5},{5,6},{6,7},{8,9},{9,10},{10,11},{12,13},{... | collective-permute-start | bytes 589832 | tf_op jit(solution)/shard_map/while/body/eval_jaxpr/ppermute | solution.py:14
  127.6 4.1 %collective-permute-done.21 = f32[64,6,1,128]{3,2,1,0:T(1,128)S(1)} collective-permute-done((f32[64,6,1,128]{3,2,1,0:T(1,128)S(1)}, f32[64,6,1,128]{3,2,1,0:T(1,128)S(1)}, u32[]{:S(2)}, u32[]{:S(2)}) %collective-permute-start.21) | collective-permute-done | bytes 196640 | tf_op jit(solution)/shard_map/while/body/eval_jaxpr/ppermute | solution.py:15
  (124 shorter events, 51.6 us)
Async XLA Ops:
  0.6 29.8 %copy-start = (f32[6,64,16]{1,2,0:T(8,128)S(1)}, f32[6,64,16]{1,2,0:T(8,128)}, u32[]{:S(2)}) copy-start(f32[6,64,16]{1,2,0:T(8,128)} %param.9) | copy-start | bytes 73732
  0.6 4.2 %collective-permute-start = (f32[1,64,4,4,128]{4,3,2,1,0:T(4,128)}, f32[1,64,4,4,128]{4,3,2,1,0:T(4,128)S(1)}, u32[]{:S(2)}, u32[]{:S(2)}) collective-permute-start(f32[1,64,4,4,128]{4,3,2,1,0:T(4,128)} %param.5), channel_id=1, source_target_pairs={{0,16},{1,17},{2,18},{3,19},{4,20},{5,21},{6,22},{7,23},{8,24},{9,... | collective-permute-start | bytes 1572872 | tf_op jit(solution)/shard_map/ppermute | solution.py:23
  6.3 6.7 %collective-permute-start.1 = (f32[64,1,4,128]{3,2,1,0:T(4,128)S(1)}, f32[64,1,4,128]{3,2,1,0:T(4,128)S(1)}, u32[]{:S(2)}, u32[]{:S(2)}) collective-permute-start(f32[64,1,4,128]{3,2,1,0:T(4,128)S(1)} %get-tuple-element.56), channel_id=1, source_target_pairs={{0,4},{4,8},{8,12},{1,5},{5,9},{9,13},{2,6},{6,10},{10,14},{3,7},{... | collective-permute-start | bytes 393224 | tf_op jit(solution)/shard_map/ppermute | solution.py:14
  10.6 7.2 %collective-permute-start.2 = (f32[64,1,4,128]{3,2,1,0:T(4,128)S(1)}, f32[64,1,4,128]{3,2,1,0:T(4,128)S(1)}, u32[]{:S(2)}, u32[]{:S(2)}) collective-permute-start(f32[64,1,4,128]{3,2,1,0:T(4,128)S(1)} %get-tuple-element.55), channel_id=1, source_target_pairs={{4,0},{8,4},{12,8},{5,1},{9,5},{13,9},{6,2},{10,6},{14,10},{7,3},{... | collective-permute-start | bytes 393224 | tf_op jit(solution)/shard_map/ppermute | solution.py:15
  18.1 6.8 %collective-permute-start.3 = (f32[64,6,1,128]{3,2,1,0:T(1,128)S(1)}, f32[64,6,1,128]{3,2,1,0:T(1,128)S(1)}, u32[]{:S(2)}, u32[]{:S(2)}) collective-permute-start(f32[64,6,1,128]{3,2,1,0:T(1,128)S(1)} %get-tuple-element.35), channel_id=1, source_target_pairs={{0,1},{1,2},{2,3},{4,5},{5,6},{6,7},{8,9},{9,10},{10,11},{12,13},{... | collective-permute-start | bytes 589832 | tf_op jit(solution)/shard_map/ppermute | solution.py:14
  21.6 7.6 %collective-permute-start.4 = (f32[64,6,1,128]{3,2,1,0:T(1,128)S(1)}, f32[64,6,1,128]{3,2,1,0:T(1,128)S(1)}, u32[]{:S(2)}, u32[]{:S(2)}) collective-permute-start(f32[64,6,1,128]{3,2,1,0:T(1,128)S(1)} %get-tuple-element.36), channel_id=1, source_target_pairs={{1,0},{2,1},{3,2},{5,4},{6,5},{7,6},{9,8},{10,9},{11,10},{13,12},{... | collective-permute-start | bytes 589832 | tf_op jit(solution)/shard_map/ppermute | solution.py:15
  32.6 6.4 %collective-permute-start.5 = (f32[64,1,4,128]{3,2,1,0:T(4,128)S(1)}, f32[64,1,4,128]{3,2,1,0:T(4,128)S(1)}, u32[]{:S(2)}, u32[]{:S(2)}) collective-permute-start(f32[64,1,4,128]{3,2,1,0:T(4,128)S(1)} %get-tuple-element.52), channel_id=1, source_target_pairs={{0,4},{4,8},{8,12},{1,5},{5,9},{9,13},{2,6},{6,10},{10,14},{3,7},{... | collective-permute-start | bytes 393224 | tf_op jit(solution)/shard_map/ppermute | solution.py:14
  36.6 6.9 %collective-permute-start.6 = (f32[64,1,4,128]{3,2,1,0:T(4,128)S(1)}, f32[64,1,4,128]{3,2,1,0:T(4,128)S(1)}, u32[]{:S(2)}, u32[]{:S(2)}) collective-permute-start(f32[64,1,4,128]{3,2,1,0:T(4,128)S(1)} %get-tuple-element.51), channel_id=1, source_target_pairs={{4,0},{8,4},{12,8},{5,1},{9,5},{13,9},{6,2},{10,6},{14,10},{7,3},{... | collective-permute-start | bytes 393224 | tf_op jit(solution)/shard_map/ppermute | solution.py:15
  43.7 6.7 %collective-permute-start.7 = (f32[64,6,1,128]{3,2,1,0:T(1,128)S(1)}, f32[64,6,1,128]{3,2,1,0:T(1,128)S(1)}, u32[]{:S(2)}, u32[]{:S(2)}) collective-permute-start(f32[64,6,1,128]{3,2,1,0:T(1,128)S(1)} %get-tuple-element.33), channel_id=1, source_target_pairs={{0,1},{1,2},{2,3},{4,5},{5,6},{6,7},{8,9},{9,10},{10,11},{12,13},{... | collective-permute-start | bytes 589832 | tf_op jit(solution)/shard_map/ppermute | solution.py:14
  47.2 7.6 %collective-permute-start.8 = (f32[64,6,1,128]{3,2,1,0:T(1,128)S(1)}, f32[64,6,1,128]{3,2,1,0:T(1,128)S(1)}, u32[]{:S(2)}, u32[]{:S(2)}) collective-permute-start(f32[64,6,1,128]{3,2,1,0:T(1,128)S(1)} %get-tuple-element.34), channel_id=1, source_target_pairs={{1,0},{2,1},{3,2},{5,4},{6,5},{7,6},{9,8},{10,9},{11,10},{13,12},{... | collective-permute-start | bytes 589832 | tf_op jit(solution)/shard_map/ppermute | solution.py:15
  58.1 6.9 %collective-permute-start.10 = (f32[64,1,4,128]{3,2,1,0:T(4,128)S(1)}, f32[64,1,4,128]{3,2,1,0:T(4,128)S(1)}, u32[]{:S(2)}, u32[]{:S(2)}) collective-permute-start(f32[64,1,4,128]{3,2,1,0:T(4,128)S(1)} %get-tuple-element.47), channel_id=1, source_target_pairs={{4,0},{8,4},{12,8},{5,1},{9,5},{13,9},{6,2},{10,6},{14,10},{7,3},{... | collective-permute-start | bytes 393224 | tf_op jit(solution)/shard_map/ppermute | solution.py:15
  59.4 7.1 %collective-permute-start.9 = (f32[64,1,4,128]{3,2,1,0:T(4,128)S(1)}, f32[64,1,4,128]{3,2,1,0:T(4,128)S(1)}, u32[]{:S(2)}, u32[]{:S(2)}) collective-permute-start(f32[64,1,4,128]{3,2,1,0:T(4,128)S(1)} %get-tuple-element.48), channel_id=1, source_target_pairs={{0,4},{4,8},{8,12},{1,5},{5,9},{9,13},{2,6},{6,10},{10,14},{3,7},{... | collective-permute-start | bytes 393224 | tf_op jit(solution)/shard_map/ppermute | solution.py:14
  66.8 6.7 %collective-permute-start.11 = (f32[64,6,1,128]{3,2,1,0:T(1,128)S(1)}, f32[64,6,1,128]{3,2,1,0:T(1,128)S(1)}, u32[]{:S(2)}, u32[]{:S(2)}) collective-permute-start(f32[64,6,1,128]{3,2,1,0:T(1,128)S(1)} %get-tuple-element.31), channel_id=1, source_target_pairs={{0,1},{1,2},{2,3},{4,5},{5,6},{6,7},{8,9},{9,10},{10,11},{12,13},{... | collective-permute-start | bytes 589832 | tf_op jit(solution)/shard_map/ppermute | solution.py:14
  70.3 7.6 %collective-permute-start.12 = (f32[64,6,1,128]{3,2,1,0:T(1,128)S(1)}, f32[64,6,1,128]{3,2,1,0:T(1,128)S(1)}, u32[]{:S(2)}, u32[]{:S(2)}) collective-permute-start(f32[64,6,1,128]{3,2,1,0:T(1,128)S(1)} %get-tuple-element.32), channel_id=1, source_target_pairs={{1,0},{2,1},{3,2},{5,4},{6,5},{7,6},{9,8},{10,9},{11,10},{13,12},{... | collective-permute-start | bytes 589832 | tf_op jit(solution)/shard_map/ppermute | solution.py:15
  81.2 6.9 %collective-permute-start.13 = (f32[64,1,4,128]{3,2,1,0:T(4,128)S(1)}, f32[64,1,4,128]{3,2,1,0:T(4,128)S(1)}, u32[]{:S(2)}, u32[]{:S(2)}) collective-permute-start(f32[64,1,4,128]{3,2,1,0:T(4,128)S(1)} %get-tuple-element.44), channel_id=1, source_target_pairs={{0,4},{4,8},{8,12},{1,5},{5,9},{9,13},{2,6},{6,10},{10,14},{3,7},{... | collective-permute-start | bytes 393224 | tf_op jit(solution)/shard_map/ppermute | solution.py:14
  85.6 8.1 %collective-permute-start.14 = (f32[64,1,4,128]{3,2,1,0:T(4,128)S(1)}, f32[64,1,4,128]{3,2,1,0:T(4,128)S(1)}, u32[]{:S(2)}, u32[]{:S(2)}) collective-permute-start(f32[64,1,4,128]{3,2,1,0:T(4,128)S(1)} %get-tuple-element.43), channel_id=1, source_target_pairs={{4,0},{8,4},{12,8},{5,1},{9,5},{13,9},{6,2},{10,6},{14,10},{7,3},{... | collective-permute-start | bytes 393224 | tf_op jit(solution)/shard_map/ppermute | solution.py:15
  94.0 5.1 %collective-permute-start.15 = (f32[64,6,1,128]{3,2,1,0:T(1,128)S(1)}, f32[64,6,1,128]{3,2,1,0:T(1,128)S(1)}, u32[]{:S(2)}, u32[]{:S(2)}) collective-permute-start(f32[64,6,1,128]{3,2,1,0:T(1,128)S(1)} %get-tuple-element.29), channel_id=1, source_target_pairs={{0,1},{1,2},{2,3},{4,5},{5,6},{6,7},{8,9},{9,10},{10,11},{12,13},{... | collective-permute-start | bytes 589832 | tf_op jit(solution)/shard_map/ppermute | solution.py:14
  95.9 7.6 %collective-permute-start.16 = (f32[64,6,1,128]{3,2,1,0:T(1,128)S(1)}, f32[64,6,1,128]{3,2,1,0:T(1,128)S(1)}, u32[]{:S(2)}, u32[]{:S(2)}) collective-permute-start(f32[64,6,1,128]{3,2,1,0:T(1,128)S(1)} %get-tuple-element.30), channel_id=1, source_target_pairs={{1,0},{2,1},{3,2},{5,4},{6,5},{7,6},{9,8},{10,9},{11,10},{13,12},{... | collective-permute-start | bytes 589832 | tf_op jit(solution)/shard_map/ppermute | solution.py:15
  106.7 31.5 %copy-start.3 = (f32[64,4,4,128]{3,2,1,0:T(4,128)}, f32[64,4,4,128]{3,2,1,0:T(4,128)S(1)}, u32[]{:S(2)}) copy-start(f32[64,4,4,128]{3,2,1,0:T(4,128)S(1)} %fusion.1) | copy-start | bytes 1572868
  106.7 2.8 %collective-permute-start.17 = (f32[64,4,4,128]{3,2,1,0:T(4,128)S(1)}, f32[64,4,4,128]{3,2,1,0:T(4,128)S(1)}, u32[]{:S(2)}, u32[]{:S(2)}) collective-permute-start(f32[64,4,4,128]{3,2,1,0:T(4,128)S(1)} %fusion.1), channel_id=1, source_target_pairs={{0,16},{1,17},{2,18},{3,19},{4,20},{5,21},{6,22},{7,23},{8,24},{9,... | collective-permute-start | bytes 1572872 | tf_op jit(solution)/shard_map/while/body/eval_jaxpr/ppermute | solution.py:23
  109.6 8.1 %collective-permute-start.18 = (f32[64,1,4,128]{3,2,1,0:T(4,128)S(1)}, f32[64,1,4,128]{3,2,1,0:T(4,128)S(1)}, u32[]{:S(2)}, u32[]{:S(2)}) collective-permute-start(f32[64,1,4,128]{3,2,1,0:T(4,128)S(1)} %get-tuple-element.40), channel_id=1, source_target_pairs={{0,4},{4,8},{8,12},{1,5},{5,9},{9,13},{2,6},{6,10},{10,14},{3,7},{... | collective-permute-start | bytes 393224 | tf_op jit(solution)/shard_map/while/body/eval_jaxpr/ppermute | solution.py:14
  114.4 7.4 %collective-permute-start.19 = (f32[64,1,4,128]{3,2,1,0:T(4,128)S(1)}, f32[64,1,4,128]{3,2,1,0:T(4,128)S(1)}, u32[]{:S(2)}, u32[]{:S(2)}) collective-permute-start(f32[64,1,4,128]{3,2,1,0:T(4,128)S(1)} %get-tuple-element.39), channel_id=1, source_target_pairs={{4,0},{8,4},{12,8},{5,1},{9,5},{13,9},{6,2},{10,6},{14,10},{7,3},{... | collective-permute-start | bytes 393224 | tf_op jit(solution)/shard_map/while/body/eval_jaxpr/ppermute | solution.py:15
  122.2 5.5 %collective-permute-start.20 = (f32[64,6,1,128]{3,2,1,0:T(1,128)S(1)}, f32[64,6,1,128]{3,2,1,0:T(1,128)S(1)}, u32[]{:S(2)}, u32[]{:S(2)}) collective-permute-start(f32[64,6,1,128]{3,2,1,0:T(1,128)S(1)} %get-tuple-element.27), channel_id=1, source_target_pairs={{0,1},{1,2},{2,3},{4,5},{5,6},{6,7},{8,9},{9,10},{10,11},{12,13},{... | collective-permute-start | bytes 589832 | tf_op jit(solution)/shard_map/while/body/eval_jaxpr/ppermute | solution.py:14
  124.1 7.7 %collective-permute-start.21 = (f32[64,6,1,128]{3,2,1,0:T(1,128)S(1)}, f32[64,6,1,128]{3,2,1,0:T(1,128)S(1)}, u32[]{:S(2)}, u32[]{:S(2)}) collective-permute-start(f32[64,6,1,128]{3,2,1,0:T(1,128)S(1)} %get-tuple-element.28), channel_id=1, source_target_pairs={{1,0},{2,1},{3,2},{5,4},{6,5},{7,6},{9,8},{10,9},{11,10},{13,12},{... | collective-permute-start | bytes 589832 | tf_op jit(solution)/shard_map/while/body/eval_jaxpr/ppermute | solution.py:15
  (3 other events, 3.2 us)
where the time goes:
time: 140 us; the launch traced here: 139 us
  waiting for transfers between devices  58.5 us (42%)
  starting transfers between devices  53.2 us (38%)
  local copies, waits for them, and re-layouts  11.4 us (8%)
  other arithmetic  8.5 us (6%)
  matrix products  6.27 us (4%)
  between operations  1.49 us (1%)
    ppermute x10, waiting for transfers between devices, padded_2(): after = lax.ppermute(initial, axis, down)  41.2 us
    ppermute x10, starting transfers between devices, padded_2(): before = lax.ppermute(last, axis, up)  36.2 us
    ppermute x10, waiting for transfers between devices, padded_2(): before = lax.ppermute(last, axis, up)  14.1 us
    ppermute x10, starting transfers between devices, padded_2(): after = lax.ppermute(initial, axis, down)  13.1 us
    ppermute x2, starting transfers between devices, passed_along(): lax.ppermute(value, axis, [(source, source + steps) for source in range(i...  3.85 us
    unnamed x27, local copies, waits for them, and re-layouts  3.43 us
    dot_general x5, matrix products, delta(): jnp.dot(lift_flat, stacked, precision=lax.Precision.HIGHEST, preferred_el...  3.38 us
    ppermute x2, waiting for transfers between devices, passed_along(): lax.ppermute(value, axis, [(source, source + steps) for source in range(i...  3.18 us
  transfers between devices with their start and end apart: 22, of which 22 were waited for; matrix products, arithmetic and copies ran while one was open for 2% of the time, Pallas kernels for 0%

commit v1 on v0

v1 whole, which is shorter than its diff:
```python
import functools

import jax
import jax.numpy as jnp
from jax import lax
from jax.experimental import pallas as pl
from jax.experimental.pallas import tpu as pltpu
from jax.sharding import PartitionSpec as P

MESH = pl.DeviceIdType.MESH
F32, BF16 = jnp.float32, jnp.bfloat16
STEPS = 4
LANES = 128


def halves(value):
    high = value.astype(BF16)
    return high, (value - high.astype(F32)).astype(BF16)


def kernel(
    counts, nx, ny,
    state_hbm, force_hbm, init_hbm, vol_ref, lift_ref,
    corr_hbm, resid_hbm,
    raw_start, raw_state, raw_force, out_c, out_r,
    fields, kept, resid, error, earlier,
    halo_x, halo_y, sent_y, s_high, s_low,
    load_sem, face_send, face_recv, start_send, start_recv, err_send, err_recv, out_sem,
):
    n_tm, n_sx, n_sy = counts
    cells = nx * ny
    tm, sx, sy = lax.axis_index("tm"), lax.axis_index("sx"), lax.axis_index("sy")
    first, more = tm == 0, tm < n_tm - 1
    exists = (sx < n_sx - 1, sx > 0, sy < n_sy - 1, sy > 0)
    comes = (sx > 0, sx < n_sx - 1, sy > 0, sy < n_sy - 1)
    shifts = ((1, 0), (-1, 0), (0, 1), (0, -1))

    def place(dt, f):
        dx, dy = shifts[f]
        return {"tm": tm + dt, "sx": sx + dx, "sy": sy + dy}

    load_state = pltpu.make_async_copy(state_hbm, raw_state, load_sem.at[0])
    load_force = pltpu.make_async_copy(force_hbm, raw_force, load_sem.at[1])
    load_init = pltpu.make_async_copy(init_hbm, raw_start, load_sem.at[2])

    @pl.when(first)
    def _():
        load_init.start()

    load_state.start()
    load_force.start()

    barrier = pltpu.get_barrier_semaphore()

    def greet(dt, f):
        pl.semaphore_signal(barrier, inc=1, device_id=place(dt, f), device_id_type=MESH)

    for f in range(4):
        pl.when(exists[f])(functools.partial(greet, 0, f))
        pl.when(exists[f] & (tm > 0))(functools.partial(greet, -1, f))

    @pl.when(tm > 0)
    def _():
        pl.semaphore_signal(
            barrier, inc=1, device_id={"tm": tm - 1, "sx": sx, "sy": sy}, device_id_type=MESH
        )

    row = lax.broadcasted_iota(jnp.int32, (64, 64), 0)
    column = lax.broadcasted_iota(jnp.int32, (64, 64), 1)
    weight = vol_ref[...] - jnp.where(row == column, 0.1, 0.0).astype(F32)
    matrix = jnp.concatenate([weight] + [lift_ref[f] for f in range(6)], axis=1)
    a_high, a_low = halves(matrix)
    a_both = jnp.concatenate([a_high, a_low], axis=0)
    face_matrix = []
    for f in range(4):
        high, low = halves(lift_ref[f])
        face_matrix.append(
            jnp.concatenate([high.astype(F32), high.astype(F32), low.astype(F32)], axis=1).astype(BF16)
        )

    wide, tall = ny * LANES, cells * LANES
    for stack in (s_high, s_low):
        stack[64:80, 0:wide] = jnp.zeros((16, wide), BF16)
        stack[80:96, tall - wide : tall] = jnp.zeros((16, wide), BF16)
        for x in range(nx):
            low, high = x * wide, (x + 1) * wide
            stack[96:112, low : low + LANES] = jnp.zeros((16, LANES), BF16)
            stack[112:128, high - LANES : high] = jnp.zeros((16, LANES), BF16)

    def no_halo(f):
        ref = (halo_x, halo_x, halo_y, halo_y)[f]
        for phase in range(STEPS + 1):
            ref[phase, f % 2] = jnp.zeros(ref.shape[2:], F32)

    for f in range(4):
        pl.when(jnp.logical_not(comes[f]))(functools.partial(no_halo, f))

    total = sum(e.astype(jnp.int32) for e in exists)
    pl.semaphore_wait(barrier, total + jnp.where(more, total + 1, 0))

    start_copy = pltpu.make_async_remote_copy(
        src_ref=state_hbm, dst_ref=raw_start, send_sem=start_send, recv_sem=start_recv,
        device_id={"tm": tm + 1, "sx": sx, "sy": sy}, device_id_type=MESH,
    )

    @pl.when(more)
    def _():
        start_copy.start()

    top = lax.broadcasted_iota(jnp.int32, (8, LANES), 0) < 4
    lane = lax.broadcasted_iota(jnp.int32, (16, LANES), 1)

    def y_plus(ref, cell):
        parts = []
        for p in range(0, 64, 32):
            one, two = ref[cell, p + 8 : p + 16, :], ref[cell, p + 24 : p + 32, :]
            parts.append(jnp.where(top, pltpu.roll(one, 4, 0), two))
        return jnp.concatenate(parts, axis=0)

    def y_minus(ref, cell):
        parts = []
        for p in range(0, 64, 32):
            one, two = ref[cell, p : p + 8, :], ref[cell, p + 16 : p + 24, :]
            parts.append(jnp.where(top, one, pltpu.roll(two, 4, 0)))
        return jnp.concatenate(parts, axis=0)

    def face_copy(ref, slot, phase, dt, f, to=None):
        if f == 0:
            src = ref.at[pl.ds(cells - ny, ny), pl.ds(48, 16), :]
        elif f == 1:
            src = ref.at[pl.ds(0, ny), pl.ds(0, 16), :]
        else:
            src = sent_y.at[slot, f - 2]
        target = (halo_x, halo_x, halo_y, halo_y)[f].at[phase, f % 2]
        return pltpu.make_async_remote_copy(
            src_ref=src, dst_ref=target,
            send_sem=face_send.at[slot, f], recv_sem=face_recv.at[phase, f],
            device_id=place(dt, f if to is None else to), device_id_type=MESH,
        )

    def send_faces(ref, slot, phase, dt):
        for f in range(2):
            pl.when(exists[f])(face_copy(ref, slot, phase, dt, f).start)
        for x in range(nx):
            sent_y[slot, 0, x] = y_plus(ref, x * ny + ny - 1)
            sent_y[slot, 1, x] = y_minus(ref, x * ny)
        for f in range(2, 4):
            pl.when(exists[f])(face_copy(ref, slot, phase, dt, f).start)

    def sent_faces(ref, slot, phase, dt):
        for f in range(4):
            pl.when(exists[f])(face_copy(ref, slot, phase, dt, f).wait_send)

    def reorder(raw, ref):
        for cell in range(cells):
            ref[cell] = raw[pl.ds(cell, 64, stride=cells), :]

    def inside(ref, finish):
        def put(rows, cell, value):
            high, low = halves(value)
            cols = slice(cell * LANES, (cell + 1) * LANES)
            s_high[rows : rows + value.shape[0], cols] = high
            s_low[rows : rows + value.shape[0], cols] = low

        for x in range(nx):
            for y in range(ny):
                cell = x * ny + y
                put(0, cell, ref[cell])
                if x + 1 < nx:
                    put(64, cell + ny, ref[cell, 48:64, :])
                if x > 0:
                    put(80, cell - ny, ref[cell, 0:16, :])
                if y + 1 < ny:
                    put(96, cell + 1, y_plus(ref, cell))
                if y > 0:
                    put(112, cell - 1, y_minus(ref, cell))
                up = pltpu.roll(ref[cell, pl.ds(3, 16, stride=4), :], 1, 1)
                put(128, cell, jnp.where(lane == 0, 0.0, up))
                down = pltpu.roll(ref[cell, pl.ds(0, 16, stride=4), :], LANES - 1, 1)
                put(144, cell, jnp.where(lane == LANES - 1, 0.0, down))
        for x in range(nx):
            cols = slice(x * wide, (x + 1) * wide)
            both = jnp.dot(a_both, s_high[:, cols], preferred_element_type=F32)
            rest = jnp.dot(a_high, s_low[:, cols], preferred_element_type=F32)
            delta = both[:64] + both[64:] + rest
            for y in range(ny):
                finish(x * ny + y, delta[:, y * LANES : (y + 1) * LANES])

    def outside(phase, out, scale):
        for f in range(4):
            pl.when(comes[f])(face_copy(kept, STEPS + 1, phase, 0, f, f ^ 1).wait_recv)
        for f in range(4):
            ref = (halo_x, halo_x, halo_y, halo_y)[f]
            count = ref.shape[2]
            trace = jnp.concatenate([ref[phase, f % 2, i] for i in range(count)], axis=1)
            high, low = halves(trace)
            added = jnp.dot(
                face_matrix[f], jnp.concatenate([high, low, high], axis=0), preferred_element_type=F32
            )
            if scale != 1.0:
                added = scale * added
            for i in range(count):
                cell = (i, cells - ny + i, i * ny, i * ny + ny - 1)[f]
                out[cell] = out[cell] + added[:, i * LANES : (i + 1) * LANES]

    @pl.when(first)
    def _():
        load_init.wait()
        reorder(raw_start, fields.at[0])
        send_faces(fields.at[0], 0, 0, 0)

    load_state.wait()
    reorder(raw_state, kept)

    @pl.when(more)
    def _():
        send_faces(kept, STEPS + 1, 0, 1)

    load_force.wait()

    @pl.when(jnp.logical_not(first))
    def _():
        start_copy.wait_recv()
        reorder(raw_start, fields.at[0])

    for step in range(STEPS):
        now = fields.at[step]
        last = step == STEPS - 1
        out = resid if last else fields.at[step + 1]
        if step > 0:
            send_faces(now, step, step, 0)

        def finish(cell, delta, now=now, out=out, last=last):
            value = now[cell] + delta + raw_force[pl.ds(cell, 64, stride=cells), :]
            out[cell] = value - kept[cell] if last else value

        inside(now, finish)
        outside(step, out, 1.0)

    def err_copy(x):
        part = pl.ds(x * ny, ny)
        return pltpu.make_async_remote_copy(
            src_ref=error.at[part], dst_ref=earlier.at[part],
            send_sem=err_send.at[x], recv_sem=err_recv.at[x],
            device_id={"tm": tm + 1, "sx": sx, "sy": sy}, device_id_type=MESH,
        )

    @pl.when(first)
    def _():
        for cell in range(cells):
            error[cell] = resid[cell]

    def store_resid():
        for cell in range(cells):
            out_r[pl.ds(cell, 64, stride=cells), :] = resid[cell]
        pltpu.make_async_copy(out_r, resid_hbm, out_sem.at[0]).start()

    @pl.when(jnp.logical_not(first))
    def _():
        store_resid()
        for x in range(nx):
            err_copy(x).wait_recv()

        def finish(cell, delta):
            error[cell] = resid[cell] + earlier[cell] + 4.0 * delta

        inside(earlier, finish)
        outside(STEPS, error, 4.0)

    @pl.when(more)
    def _():
        for x in range(nx):
            err_copy(x).start()
        send_faces(error, STEPS, STEPS, 1)

    pl.when(first)(store_resid)
    for cell in range(cells):
        out_c[pl.ds(cell, 64, stride=cells), :] = kept[cell] + error[cell]
    store = pltpu.make_async_copy(out_c, corr_hbm, out_sem.at[1])
    store.start()

    @pl.when(first)
    def _():
        sent_faces(fields.at[0], 0, 0, 0)

    for step in range(1, STEPS):
        sent_faces(fields.at[step], step, step, 0)

    @pl.when(more)
    def _():
        start_copy.wait_send()
        sent_faces(kept, STEPS + 1, 0, 1)
        for x in range(nx):
            err_copy(x).wait_send()
        sent_faces(error, STEPS, STEPS, 1)

    pltpu.make_async_copy(out_r, resid_hbm, out_sem.at[0]).wait()
    store.wait()


def solution(mesh):
    counts = tuple(mesh.shape[axis] for axis in ("tm", "sx", "sy"))

    def local(slices_state, forcing, initial, volume, lift):
        _, dofs, nx, ny, nz = slices_state.shape
        cells = nx * ny
        rows = dofs * cells
        raw = pltpu.VMEM((rows, nz), F32)
        field = pltpu.VMEM((cells, dofs, nz), F32)
        stack = pltpu.VMEM((160, cells * nz), BF16)
        flat = jax.ShapeDtypeStruct((rows, nz), F32)
        corrected, residual = pl.pallas_call(
            functools.partial(kernel, counts, nx, ny),
            out_shape=(flat, flat),
            in_specs=[pl.BlockSpec(memory_space=pl.ANY)] * 3
            + [pl.BlockSpec(memory_space=pltpu.VMEM)] * 2,
            out_specs=(pl.BlockSpec(memory_space=pl.ANY),) * 2,
            scratch_shapes=[
                raw, raw, raw, raw, raw,
                pltpu.VMEM((STEPS, cells, dofs, nz), F32), field, field, field, field,
                pltpu.VMEM((STEPS + 1, 2, ny, 16, nz), F32),
                pltpu.VMEM((STEPS + 1, 2, nx, 16, nz), F32),
                pltpu.VMEM((STEPS + 2, 2, nx, 16, nz), F32),
                stack, stack,
                pltpu.SemaphoreType.DMA((3,)),
                pltpu.SemaphoreType.DMA((STEPS + 2, 4)),
                pltpu.SemaphoreType.DMA((STEPS + 1, 4)),
                pltpu.SemaphoreType.DMA,
                pltpu.SemaphoreType.DMA,
                pltpu.SemaphoreType.DMA((nx,)),
                pltpu.SemaphoreType.DMA((nx,)),
                pltpu.SemaphoreType.DMA((2,)),
            ],
            compiler_params=pltpu.CompilerParams(
                collective_id=0, has_side_effects=True, vmem_limit_bytes=32 * 2**20
            ),
            name="cycle",
        )(
            slices_state.reshape(rows, nz), forcing.reshape(rows, nz), initial.reshape(rows, nz),
            volume, lift,
        )
        shape = slices_state.shape
        return corrected.reshape(shape), residual.reshape(shape)

    split = P("tm", None, "sx", "sy", None)
    return jax.shard_map(
        local,
        mesh=mesh,
        in_specs=(split, split, P(None, "sx", "sy", None), P(), P()),
        out_specs=(split, split),
        check_vma=False,
    )
```

time: 140 us -> 29.7 us (0.21)
  the two profiles are of different devices: /device:TPU:0 before, /device:TPU:1 now
where the time goes in v1:
time: 29.7 us; the launch traced here: 29.4 us
  Pallas kernels  23.1 us (78%)
  local copies, waits for them, and re-layouts  5.62 us (19%)
  between operations  0.67 us (2%)
    pallas_call x1, Pallas kernels, local(): pl.pallas_call(functools.partial(kernel, counts, nx, ny), out_shape=(flat...  23.1 us
    unnamed x11, local copies, waits for them, and re-layouts  5.62 us

profile of v1, /device:TPU:1, one launch (start us, length us, event | category | flops | bytes accessed | tf_op | source)
XLA Modules:
  0.0 29.4 jit_solution(2188933338454185605)
XLA Ops:
  0.6 0.0 copy-start.3
  0.6 0.9 %copy.7.lift_ref = f32[6,64,16]{2,1,0:T(8,128)S(1)} copy(f32[6,64,16]{1,2,0:T(8,128)} %param.9) | data formatting | bytes 49152 | tf_op args[4]
  1.6 0.0 copy-done.3
  1.6 0.0 copy-start
  1.6 1.0 %copy-done = f32[1,64,4,4,128]{4,3,2,1,0:T(4,128)S(1)} copy-done((f32[1,64,4,4,128]{4,3,2,1,0:T(4,128)S(1)}, f32[1,64,4,4,128]{4,3,2,1,0:T(4,128)}, u32[]{:S(2)}) %copy-start) | copy-done | bytes 524312
  2.6 0.0 copy-start.1
  2.6 1.0 %copy-done.1 = f32[1,64,4,4,128]{4,3,2,1,0:T(4,128)S(1)} copy-done((f32[1,64,4,4,128]{4,3,2,1,0:T(4,128)S(1)}, f32[1,64,4,4,128]{4,3,2,1,0:T(4,128)}, u32[]{:S(2)}) %copy-start.1) | copy-done | bytes 524312
  3.7 0.0 copy-start.2
  3.7 1.0 %copy-done.2 = f32[64,4,4,128]{3,2,1,0:T(4,128)S(1)} copy-done((f32[64,4,4,128]{3,2,1,0:T(4,128)S(1)}, f32[64,4,4,128]{3,2,1,0:T(4,128)}, u32[]{:S(2)}) %copy-start.2) | copy-done | bytes 524312
  4.7 23.1 %cycle.1 = (f32[1024,128]{1,0:T(8,128)S(1)}, f32[1024,128]{1,0:T(8,128)S(1)}) custom-call(f32[1024,128]{1,0:T(8,128)S(1)} %bitcast.5, f32[1024,128]{1,0:T(8,128)S(1)} %bitcast.6, f32[1024,128]{1,0:T(8,128)S(1)} %bitcast.7, f32[64,64]{1,0:T(8,128)S(1)} %copy-done.3, f32[6,64,16]{2,1,0:T(8,128)S(1)} %copy.7.lift_ref), custom_call_target="tpu_custom_call" | custom-call | tf_op jit(solution)/shard_map/cycle/pallas_call | solution.py:312
  27.8 0.8 %copy.10 = f32[1,64,4,4,128]{4,3,2,1,0:T(4,128)} copy(f32[1,64,4,4,128]{4,3,2,1,0:T(4,128)S(1)} %bitcast.9) | data formatting | bytes 1048576
  28.6 0.8 %copy.11 = f32[1,64,4,4,128]{4,3,2,1,0:T(4,128)} copy(f32[1,64,4,4,128]{4,3,2,1,0:T(4,128)S(1)} %bitcast.8) | data formatting | bytes 1048576
Async XLA Ops:
  0.6 0.9 %copy-start.3 = (f32[64,64]{1,0:T(8,128)S(1)}, f32[64,64]{1,0:T(8,128)}, u32[]{:S(2)}) copy-start(f32[64,64]{1,0:T(8,128)} %vol_ref.1) | copy-start | bytes 49156
  1.6 1.0 %copy-start = (f32[1,64,4,4,128]{4,3,2,1,0:T(4,128)S(1)}, f32[1,64,4,4,128]{4,3,2,1,0:T(4,128)}, u32[]{:S(2)}) copy-start(f32[1,64,4,4,128]{4,3,2,1,0:T(4,128)} %param.5) | copy-start | bytes 1572868
  2.6 1.0 %copy-start.1 = (f32[1,64,4,4,128]{4,3,2,1,0:T(4,128)S(1)}, f32[1,64,4,4,128]{4,3,2,1,0:T(4,128)}, u32[]{:S(2)}) copy-start(f32[1,64,4,4,128]{4,3,2,1,0:T(4,128)} %param.6) | copy-start | bytes 1572868
  3.7 1.0 %copy-start.2 = (f32[64,4,4,128]{3,2,1,0:T(4,128)S(1)}, f32[64,4,4,128]{3,2,1,0:T(4,128)}, u32[]{:S(2)}) copy-start(f32[64,4,4,128]{3,2,1,0:T(4,128)} %param.7) | copy-start | bytes 1572868

commit v2 on v1

--- a/solution.py
+++ b/solution.py
@@ -20,12 +20,12 @@
 
 def kernel(
     counts, nx, ny,
-    state_hbm, force_hbm, init_hbm, vol_ref, lift_ref,
-    corr_hbm, resid_hbm,
-    raw_start, raw_state, raw_force, out_c, out_r,
-    fields, kept, resid, error, earlier,
+    state_hbm, force_hbm, init_hbm, vol_hbm, lift_hbm,
+    kept, resid, error,
+    raw_start, raw_state, raw_force, volume, lift,
+    fields, source, earlier,
     halo_x, halo_y, sent_y, s_high, s_low,
-    load_sem, face_send, face_recv, start_send, start_recv, err_send, err_recv, out_sem,
+    load_sem, face_send, face_recv, start_send, start_recv, err_send, err_recv,
 ):
     n_tm, n_sx, n_sy = counts
     cells = nx * ny
@@ -49,6 +49,10 @@
 
     load_state.start()
     load_force.start()
+    load_volume = pltpu.make_async_copy(vol_hbm, volume, load_sem.at[3])
+    load_lift = pltpu.make_async_copy(lift_hbm, lift, load_sem.at[4])
+    load_volume.start()
+    load_lift.start()
 
     barrier = pltpu.get_barrier_semaphore()
 
@@ -63,19 +67,6 @@
     def _():
         pl.semaphore_signal(
             barrier, inc=1, device_id={"tm": tm - 1, "sx": sx, "sy": sy}, device_id_type=MESH
-        )
-
-    row = lax.broadcasted_iota(jnp.int32, (64, 64), 0)
-    column = lax.broadcasted_iota(jnp.int32, (64, 64), 1)
-    weight = vol_ref[...] - jnp.where(row == column, 0.1, 0.0).astype(F32)
-    matrix = jnp.concatenate([weight] + [lift_ref[f] for f in range(6)], axis=1)
-    a_high, a_low = halves(matrix)
-    a_both = jnp.concatenate([a_high, a_low], axis=0)
-    face_matrix = []
-    for f in range(4):
-        high, low = halves(lift_ref[f])
-        face_matrix.append(
-            jnp.concatenate([high.astype(F32), high.astype(F32), low.astype(F32)], axis=1).astype(BF16)
         )
 
     wide, tall = ny * LANES, cells * LANES
@@ -98,14 +89,18 @@
     total = sum(e.astype(jnp.int32) for e in exists)
     pl.semaphore_wait(barrier, total + jnp.where(more, total + 1, 0))
 
-    start_copy = pltpu.make_async_remote_copy(
-        src_ref=state_hbm, dst_ref=raw_start, send_sem=start_send, recv_sem=start_recv,
-        device_id={"tm": tm + 1, "sx": sx, "sy": sy}, device_id_type=MESH,
-    )
+    def start_copy(x):
+        part = pl.ds(x * 64 * ny, 64 * ny)
+        return pltpu.make_async_remote_copy(
+            src_ref=state_hbm.at[part], dst_ref=raw_start.at[part],
+            send_sem=start_send.at[x], recv_sem=start_recv.at[x],
+            device_id={"tm": tm + 1, "sx": sx, "sy": sy}, device_id_type=MESH,
+        )
 
     @pl.when(more)
     def _():
-        start_copy.start()
+        for x in range(nx):
+            start_copy(x).start()
 
     top = lax.broadcasted_iota(jnp.int32, (8, LANES), 0) < 4
     lane = lax.broadcasted_iota(jnp.int32, (16, LANES), 1)
@@ -165,11 +160,13 @@
         for x in range(nx):
             for y in range(ny):
                 cell = x * ny + y
-                put(0, cell, ref[cell])
-                if x + 1 < nx:
-                    put(64, cell + ny, ref[cell, 48:64, :])
-                if x > 0:
-                    put(80, cell - ny, ref[cell, 0:16, :])
+                pair = halves(ref[cell])
+                for stack, half in zip((s_high, s_low), pair):
+                    stack[0:64, cell * LANES : (cell + 1) * LANES] = half
+                    if x + 1 < nx:
+                        stack[64:80, (cell + ny) * LANES : (cell + ny + 1) * LANES] = half[48:64]
+                    if x > 0:
+                        stack[80:96, (cell - ny) * LANES : (cell - ny + 1) * LANES] = half[0:16]
                 if y + 1 < ny:
                     put(96, cell + 1, y_plus(ref, cell))
                 if y > 0:
@@ -217,10 +214,27 @@
         send_faces(kept, STEPS + 1, 0, 1)
 
     load_force.wait()
+    reorder(raw_force, source)
+
+    load_volume.wait()
+    load_lift.wait()
+    row = lax.broadcasted_iota(jnp.int32, (64, 64), 0)
+    column = lax.broadcasted_iota(jnp.int32, (64, 64), 1)
+    weight = volume[...] - jnp.where(row == column, 0.1, 0.0).astype(F32)
+    lifts = jnp.concatenate([lift[f] for f in range(6)], axis=0).T
+    a_high, a_low = halves(jnp.concatenate([weight, lifts], axis=1))
+    a_both = jnp.concatenate([a_high, a_low], axis=0)
+    face_matrix = []
+    for f in range(4):
+        high, low = halves(lifts[:, 16 * f : 16 * f + 16])
+        face_matrix.append(
+            jnp.concatenate([high.astype(F32), high.astype(F32), low.astype(F32)], axis=1).astype(BF16)
+        )
 
     @pl.when(jnp.logical_not(first))
     def _():
-        start_copy.wait_recv()
+        for x in range(nx):
+            start_copy(x).wait_recv()
         reorder(raw_start, fields.at[0])
 
     for step in range(STEPS):
@@ -231,7 +245,7 @@
             send_faces(now, step, step, 0)
 
         def finish(cell, delta, now=now, out=out, last=last):
-            value = now[cell] + delta + raw_force[pl.ds(cell, 64, stride=cells), :]
+            value = now[cell] + delta + source[cell]
             out[cell] = value - kept[cell] if last else value
 
         inside(now, finish)
@@ -250,14 +264,8 @@
         for cell in range(cells):
             error[cell] = resid[cell]
 
-    def store_resid():
-        for cell in range(cells):
-            out_r[pl.ds(cell, 64, stride=cells), :] = resid[cell]
-        pltpu.make_async_copy(out_r, resid_hbm, out_sem.at[0]).start()
-
     @pl.when(jnp.logical_not(first))
     def _():
-        store_resid()
         for x in range(nx):
             err_copy(x).wait_recv()
 
@@ -273,12 +281,6 @@
             err_copy(x).start()
         send_faces(error, STEPS, STEPS, 1)
 
-    pl.when(first)(store_resid)
-    for cell in range(cells):
-        out_c[pl.ds(cell, 64, stride=cells), :] = kept[cell] + error[cell]
-    store = pltpu.make_async_copy(out_c, corr_hbm, out_sem.at[1])
-    store.start()
-
     @pl.when(first)
     def _():
         sent_faces(fields.at[0], 0, 0, 0)
@@ -288,14 +290,29 @@
 
     @pl.when(more)
     def _():
-        start_copy.wait_send()
         sent_faces(kept, STEPS + 1, 0, 1)
         for x in range(nx):
+            start_copy(x).wait_send()
             err_copy(x).wait_send()
         sent_faces(error, STEPS, STEPS, 1)
 
-    pltpu.make_async_copy(out_r, resid_hbm, out_sem.at[0]).wait()
-    store.wait()
+
+def finishing(nx, ny, kept, resid, error, corr_hbm, resid_hbm, out_c, out_r, out_sem):
+    cells = nx * ny
+    copies = []
+    for part in range(4):
+        low, rows = part * 16 * cells, 16 * cells
+        for cell in range(cells):
+            dofs = slice(part * 16, part * 16 + 16)
+            value = resid[cell, dofs, :]
+            out_r[pl.ds(low + cell, 16, stride=cells), :] = value
+            out_c[pl.ds(low + cell, 16, stride=cells), :] = kept[cell, dofs, :] + error[cell, dofs, :]
+        for i, (src, dst) in enumerate(((out_r, resid_hbm), (out_c, corr_hbm))):
+            span = pl.ds(low, rows)
+            copies.append(pltpu.make_async_copy(src.at[span], dst.at[span], out_sem.at[part, i]))
+            copies[-1].start()
+    for copy in copies:
+        copy.wait()
 
 
 def solution(mesh):
@@ -309,36 +326,50 @@
         field = pltpu.VMEM((cells, dofs, nz), F32)
         stack = pltpu.VMEM((160, cells * nz), BF16)
         flat = jax.ShapeDtypeStruct((rows, nz), F32)
-        corrected, residual = pl.pallas_call(
+        shaped = jax.ShapeDtypeStruct((cells, dofs, nz), F32)
+        vmem, hbm = pl.BlockSpec(memory_space=pltpu.VMEM), pl.BlockSpec(memory_space=pltpu.HBM)
+        parts = pl.pallas_call(
             functools.partial(kernel, counts, nx, ny),
-            out_shape=(flat, flat),
-            in_specs=[pl.BlockSpec(memory_space=pl.ANY)] * 3
-            + [pl.BlockSpec(memory_space=pltpu.VMEM)] * 2,
-            out_specs=(pl.BlockSpec(memory_space=pl.ANY),) * 2,
+            out_shape=(shaped,) * 3,
+            in_specs=[hbm] * 5,
+            out_specs=(vmem,) * 3,
             scratch_shapes=[
-                raw, raw, raw, raw, raw,
-                pltpu.VMEM((STEPS, cells, dofs, nz), F32), field, field, field, field,
+                raw, raw, raw, pltpu.VMEM(volume.shape, F32), pltpu.VMEM((6, 16, dofs), F32),
+                pltpu.VMEM((STEPS, cells, dofs, nz), F32), field, field,
                 pltpu.VMEM((STEPS + 1, 2, ny, 16, nz), F32),
                 pltpu.VMEM((STEPS + 1, 2, nx, 16, nz), F32),
                 pltpu.VMEM((STEPS + 2, 2, nx, 16, nz), F32),
                 stack, stack,
-                pltpu.SemaphoreType.DMA((3,)),
+                pltpu.SemaphoreType.DMA((5,)),
                 pltpu.SemaphoreType.DMA((STEPS + 2, 4)),
                 pltpu.SemaphoreType.DMA((STEPS + 1, 4)),
-                pltpu.SemaphoreType.DMA,
-                pltpu.SemaphoreType.DMA,
                 pltpu.SemaphoreType.DMA((nx,)),
                 pltpu.SemaphoreType.DMA((nx,)),
-                pltpu.SemaphoreType.DMA((2,)),
+                pltpu.SemaphoreType.DMA((nx,)),
+                pltpu.SemaphoreType.DMA((nx,)),
             ],
             compiler_params=pltpu.CompilerParams(
                 collective_id=0, has_side_effects=True, vmem_limit_bytes=32 * 2**20
             ),
             name="cycle",
         )(
-            slices_state.reshape(rows, nz), forcing.reshape(rows, nz), initial.reshape(rows, nz),
-            volume, lift,
-        )
+            *(
+                pltpu.with_memory_space_constraint(value, pltpu.HBM)
+                for value in (
+                    slices_state.reshape(rows, nz), forcing.reshape(rows, nz),
+                    initial.reshape(rows, nz), volume, jnp.swapaxes(lift, 1, 2),
+                )
+            )
+        )
+        corrected, residual = pl.pallas_call(
+            functools.partial(finishing, nx, ny),
+            out_shape=(flat,) * 2,
+            in_specs=[vmem] * 3,
+            out_specs=(hbm,) * 2,
+            scratch_shapes=[raw, raw, pltpu.SemaphoreType.DMA((4, 2))],
+            compiler_params=pltpu.CompilerParams(vmem_limit_bytes=16 * 2**20),
+            name="finishing",
+        )(*parts)
         shape = slices_state.shape
         return corrected.reshape(shape), residual.reshape(shape)
 

time: 29.7 us -> 24.6 us (0.83)
  local copies, waits for them, and re-layouts: 5.62 us -> 0 us
  Pallas kernels: 23.1 us -> 23.8 us
    unnamed x11 -> x0, local copies, waits for them, and re-layouts: 5.62 us -> none
    pallas_call x1 -> x2, Pallas kernels: 23.1 us -> 23.8 us  [the longest x1 22.8 us: local(): pl.pallas_call(functools.partial(kernel, counts, nx, ny), out_shape=(shap...]
where the time goes in v2:
time: 24.6 us; the launch traced here: 24.5 us
  Pallas kernels  23.8 us (97%)
  between operations  0.64 us (3%)
    pallas_call x1, Pallas kernels, local(): pl.pallas_call(functools.partial(kernel, counts, nx, ny), out_shape=(shap...  22.8 us
    pallas_call x1, Pallas kernels, local(): pl.pallas_call(functools.partial(finishing, nx, ny), out_shape=(flat,) *...  1.08 us

profile of v2, /device:TPU:1, one launch (start us, length us, event | category | flops | bytes accessed | tf_op | source)
XLA Modules:
  0.0 24.5 jit_solution(5611695747728410805)
XLA Ops:
  0.6 22.8 %cycle.1 = (f32[16,64,128]{2,1,0:T(8,128)S(1)}, f32[16,64,128]{2,1,0:T(8,128)S(1)}, f32[16,64,128]{2,1,0:T(8,128)S(1)}) custom-call(f32[1024,128]{1,0:T(8,128)} %bitcast.6, f32[1024,128]{1,0:T(8,128)} %bitcast.7, f32[1024,128]{1,0:T(8,128)} %bitcast.8, f32[64,64]{1,0:T(8,128)} %vol_hbm.1, f32[6,16,64]{2,1,0:T(8,128)} %bitcast.9), custom_call_target="tpu_custom_call" | custom-call | tf_op jit(solution)/shard_map/cycle/pallas_call | solution.py:331
  23.4 1.1 %finishing.1 = (f32[1024,128]{1,0:T(8,128)}, f32[1024,128]{1,0:T(8,128)}) custom-call(f32[16,64,128]{2,1,0:T(8,128)S(1)} %get-tuple-element.7.kept, f32[16,64,128]{2,1,0:T(8,128)S(1)} %get-tuple-element.8.resid, f32[16,64,128]{2,1,0:T(8,128)S(1)} %get-tuple-element.9.error), custom_call_target="tpu_custom_call" | custom-call | tf_op jit(solution)/shard_map/finishing/pallas_call | solution.py:364

commit v3 on v2

--- a/solution.py
+++ b/solution.py
@@ -134,8 +134,10 @@
         )
 
     def send_faces(ref, slot, phase, dt):
-        for f in range(2):
-            pl.when(exists[f])(face_copy(ref, slot, phase, dt, f).start)
+        odd = lax.rem(sx, 2) == 1
+        pl.when(exists[0] & odd)(face_copy(ref, slot, phase, dt, 0).start)
+        pl.when(exists[1])(face_copy(ref, slot, phase, dt, 1).start)
+        pl.when(exists[0] & jnp.logical_not(odd))(face_copy(ref, slot, phase, dt, 0).start)
         for x in range(nx):
             sent_y[slot, 0, x] = y_plus(ref, x * ny + ny - 1)
             sent_y[slot, 1, x] = y_minus(ref, x * ny)
@@ -184,21 +186,22 @@
                 finish(x * ny + y, delta[:, y * LANES : (y + 1) * LANES])
 
     def outside(phase, out, scale):
-        for f in range(4):
-            pl.when(comes[f])(face_copy(kept, STEPS + 1, phase, 0, f, f ^ 1).wait_recv)
-        for f in range(4):
-            ref = (halo_x, halo_x, halo_y, halo_y)[f]
-            count = ref.shape[2]
-            trace = jnp.concatenate([ref[phase, f % 2, i] for i in range(count)], axis=1)
-            high, low = halves(trace)
-            added = jnp.dot(
-                face_matrix[f], jnp.concatenate([high, low, high], axis=0), preferred_element_type=F32
-            )
-            if scale != 1.0:
-                added = scale * added
-            for i in range(count):
-                cell = (i, cells - ny + i, i * ny, i * ny + ny - 1)[f]
-                out[cell] = out[cell] + added[:, i * LANES : (i + 1) * LANES]
+        for faces in ((2, 3), (0, 1)):
+            for f in faces:
+                pl.when(comes[f])(face_copy(kept, STEPS + 1, phase, 0, f, f ^ 1).wait_recv)
+            for f in faces:
+                ref = (halo_x, halo_x, halo_y, halo_y)[f]
+                count = ref.shape[2]
+                trace = jnp.concatenate([ref[phase, f % 2, i] for i in range(count)], axis=1)
+                high, low = halves(trace)
+                added = jnp.dot(
+                    face_matrix[f], jnp.concatenate([high, low, high], axis=0), preferred_element_type=F32
+                )
+                if scale != 1.0:
+                    added = scale * added
+                for i in range(count):
+                    cell = (i, cells - ny + i, i * ny, i * ny + ny - 1)[f]
+                    out[cell] = out[cell] + added[:, i * LANES : (i + 1) * LANES]
 
     @pl.when(first)
     def _():
@@ -277,9 +280,9 @@
 
     @pl.when(more)
     def _():
+        send_faces(error, STEPS, STEPS, 1)
         for x in range(nx):
             err_copy(x).start()
-        send_faces(error, STEPS, STEPS, 1)
 
     @pl.when(first)
     def _():

time: 24.6 us -> 24.6 us (level)
  no operation moved by 1% of the time
where the time goes in v3:
time: 24.6 us; the launch traced here: 24.4 us
  Pallas kernels  23.8 us (97%)
  between operations  0.64 us (3%)
    pallas_call x1, Pallas kernels, local(): pl.pallas_call(functools.partial(kernel, counts, nx, ny), out_shape=(shap...  22.7 us
    pallas_call x1, Pallas kernels, local(): pl.pallas_call(functools.partial(finishing, nx, ny), out_shape=(flat,) *...  1.08 us

profile of v3, /device:TPU:1, one launch (start us, length us, event | category | flops | bytes accessed | tf_op | source)
XLA Modules:
  0.0 24.4 jit_solution(13590055414712640214)
XLA Ops:
  0.6 22.7 %cycle.1 = (f32[16,64,128]{2,1,0:T(8,128)S(1)}, f32[16,64,128]{2,1,0:T(8,128)S(1)}, f32[16,64,128]{2,1,0:T(8,128)S(1)}) custom-call(f32[1024,128]{1,0:T(8,128)} %bitcast.6, f32[1024,128]{1,0:T(8,128)} %bitcast.7, f32[1024,128]{1,0:T(8,128)} %bitcast.8, f32[64,64]{1,0:T(8,128)} %vol_hbm.1, f32[6,16,64]{2,1,0:T(8,128)} %bitcast.9), custom_call_target="tpu_custom_call" | custom-call | tf_op jit(solution)/shard_map/cycle/pallas_call | solution.py:334
  23.3 1.1 %finishing.1 = (f32[1024,128]{1,0:T(8,128)}, f32[1024,128]{1,0:T(8,128)}) custom-call(f32[16,64,128]{2,1,0:T(8,128)S(1)} %get-tuple-element.7.kept, f32[16,64,128]{2,1,0:T(8,128)S(1)} %get-tuple-element.8.resid, f32[16,64,128]{2,1,0:T(8,128)S(1)} %get-tuple-element.9.error), custom_call_target="tpu_custom_call" | custom-call | tf_op jit(solution)/shard_map/finishing/pallas_call | solution.py:367

commit v4 on v3

--- a/solution.py
+++ b/solution.py
@@ -10,6 +10,8 @@
 MESH = pl.DeviceIdType.MESH
 F32, BF16 = jnp.float32, jnp.bfloat16
 STEPS = 4
+WHOLE = (0, 2, 4)
+PAIRED = (0, 2)
 LANES = 128
 
 
@@ -24,8 +26,9 @@
     kept, resid, error,
     raw_start, raw_state, raw_force, volume, lift,
     fields, source, earlier,
-    halo_x, halo_y, sent_y, s_high, s_low,
+    halo_x, halo_y, sent_y, corner, edge, sent_edge, s_high, s_low,
     load_sem, face_send, face_recv, start_send, start_recv, err_send, err_recv,
+    corner_send, corner_recv, edge_send, edge_recv,
 ):
     n_tm, n_sx, n_sy = counts
     cells = nx * ny
@@ -34,10 +37,14 @@
     exists = (sx < n_sx - 1, sx > 0, sy < n_sy - 1, sy > 0)
     comes = (sx > 0, sx < n_sx - 1, sy > 0, sy < n_sy - 1)
     shifts = ((1, 0), (-1, 0), (0, 1), (0, -1))
+    diagonals = [(fx, fy) for fx in (0, 1) for fy in (2, 3)]
 
     def place(dt, f):
         dx, dy = shifts[f]
         return {"tm": tm + dt, "sx": sx + dx, "sy": sy + dy}
+
+    def across(dt, fx, fy):
+        return {"tm": tm + dt, "sx": sx + shifts[fx][0], "sy": sy + shifts[fy][1]}
 
     load_state = pltpu.make_async_copy(state_hbm, raw_state, load_sem.at[0])
     load_force = pltpu.make_async_copy(force_hbm, raw_force, load_sem.at[1])
@@ -63,6 +70,16 @@
         pl.when(exists[f])(functools.partial(greet, 0, f))
         pl.when(exists[f] & (tm > 0))(functools.partial(greet, -1, f))
 
+    def greet_across(dt, fx, fy):
+        pl.semaphore_signal(
+            barrier, inc=1, device_id=across(dt, fx, fy), device_id_type=MESH
+        )
+
+    for fx, fy in diagonals:
+        there = exists[fx] & exists[fy]
+        pl.when(there)(functools.partial(greet_across, 0, fx, fy))
+        pl.when(there & (tm > 0))(functools.partial(greet_across, -1, fx, fy))
+
     @pl.when(tm > 0)
     def _():
         pl.semaphore_signal(
@@ -86,7 +103,15 @@
     for f in range(4):
         pl.when(jnp.logical_not(comes[f]))(functools.partial(no_halo, f))
 
+    def no_corner(fx, fy):
+        for pair in range(STEPS // 2):
+            corner[pair, fx, fy - 2] = jnp.zeros((16, LANES), F32)
+
+    for fx, fy in diagonals:
+        pl.when(jnp.logical_not(comes[fx] & comes[fy]))(functools.partial(no_corner, fx, fy))
+
     total = sum(e.astype(jnp.int32) for e in exists)
+    total = total + sum((exists[fx] & exists[fy]).astype(jnp.int32) for fx, fy in diagonals)
     pl.semaphore_wait(barrier, total + jnp.where(more, total + 1, 0))
 
     def start_copy(x):
@@ -134,25 +159,80 @@
         )
 
     def send_faces(ref, slot, phase, dt):
-        odd = lax.rem(sx, 2) == 1
-        pl.when(exists[0] & odd)(face_copy(ref, slot, phase, dt, 0).start)
-        pl.when(exists[1])(face_copy(ref, slot, phase, dt, 1).start)
-        pl.when(exists[0] & jnp.logical_not(odd))(face_copy(ref, slot, phase, dt, 0).start)
+        if phase in WHOLE:
+            odd = lax.rem(sx, 2) == 1
+            pl.when(exists[0] & odd)(face_copy(ref, slot, phase, dt, 0).start)
+            pl.when(exists[1])(face_copy(ref, slot, phase, dt, 1).start)
+            pl.when(exists[0] & jnp.logical_not(odd))(face_copy(ref, slot, phase, dt, 0).start)
         for x in range(nx):
             sent_y[slot, 0, x] = y_plus(ref, x * ny + ny - 1)
             sent_y[slot, 1, x] = y_minus(ref, x * ny)
         for f in range(2, 4):
             pl.when(exists[f])(face_copy(ref, slot, phase, dt, f).start)
+        if phase in PAIRED:
+            for fx, fy in diagonals:
+                pl.when(exists[fx] & exists[fy])(corner_copy(slot, phase, dt, fx, fy).start)
 
     def sent_faces(ref, slot, phase, dt):
-        for f in range(4):
+        for f in range(4) if phase in WHOLE else range(2, 4):
             pl.when(exists[f])(face_copy(ref, slot, phase, dt, f).wait_send)
+        if phase in PAIRED:
+            for fx, fy in diagonals:
+                pl.when(exists[fx] & exists[fy])(corner_copy(slot, phase, dt, fx, fy).wait_send)
+
+    def corner_copy(slot, phase, dt, fx, fy, back=False):
+        cell = nx - 1 if fx == 0 else 0
+        pair = PAIRED.index(phase)
+        target = across(dt, fx ^ 1, fy ^ 1) if back else across(dt, fx, fy)
+        return pltpu.make_async_remote_copy(
+            src_ref=sent_y.at[slot, fy - 2, cell], dst_ref=corner.at[pair, fx, fy - 2],
+            send_sem=corner_send.at[slot, 2 * fx + fy - 2],
+            recv_sem=corner_recv.at[pair, 2 * fx + fy - 2],
+            device_id=target, device_id_type=MESH,
+        )
+
+    def edge_copy(pair, f, to=None):
+        return pltpu.make_async_remote_copy(
+            src_ref=sent_edge.at[pair, f], dst_ref=edge.at[pair, f],
+            send_sem=edge_send.at[pair, f], recv_sem=edge_recv.at[pair, f],
+            device_id=place(0, f if to is None else to), device_id_type=MESH,
+        )
+
+    def send_edges(pair, ref):
+        for y in range(ny):
+            sent_edge[pair, 0, y] = ref[cells - ny + y, 48:64, :]
+            sent_edge[pair, 1, y] = ref[y, 0:16, :]
+        for f in range(2):
+            pl.when(exists[f])(edge_copy(pair, f).start)
+
+    def next_faces(phase):
+        pair, now = PAIRED.index(phase), fields.at[phase]
+        for fx in range(2):
+
+            @pl.when(comes[fx])
+            def _(fx=fx):
+                edge_copy(pair, fx, fx ^ 1).wait_recv()
+                for fy in (2, 3):
+                    back = corner_copy(0, phase, 0, fx, fy, True)
+                    pl.when(comes[fy])(back.wait_recv)
+                cell, low = (0, 0) if fx == 0 else (cells - ny, 48)
+                own = [now[cell + y, low : low + 16, :] for y in range(ny)]
+                none = [jnp.zeros((16, LANES), F32)] * (ny - 1)
+                rows = []
+                for blocks in (own, [corner[pair, fx, 0]] + none, none + [corner[pair, fx, 1]]):
+                    high, part = halves(jnp.concatenate(blocks, axis=1))
+                    rows += [high, part, high]
+                added = jnp.dot(
+                    edge_matrix[fx], jnp.concatenate(rows, axis=0), preferred_element_type=F32
+                )
+                for y in range(ny):
+                    halo_x[phase + 1, fx, y] = edge[pair, fx, y] + added[:, y * LANES : (y + 1) * LANES]
 
     def reorder(raw, ref):
         for cell in range(cells):
             ref[cell] = raw[pl.ds(cell, 64, stride=cells), :]
 
-    def inside(ref, finish):
+    def inside(ref, finish, edges=None):
         def put(rows, cell, value):
             high, low = halves(value)
             cols = slice(cell * LANES, (cell + 1) * LANES)
@@ -177,7 +257,10 @@
                 put(128, cell, jnp.where(lane == 0, 0.0, up))
                 down = pltpu.roll(ref[cell, pl.ds(0, 16, stride=4), :], LANES - 1, 1)
                 put(144, cell, jnp.where(lane == LANES - 1, 0.0, down))
-        for x in range(nx):
+        order = list(dict.fromkeys([0, nx - 1] + list(range(nx))))
+        for turn, x in enumerate(order):
+            if edges is not None and turn == min(2, nx):
+                edges()
             cols = slice(x * wide, (x + 1) * wide)
             both = jnp.dot(a_both, s_high[:, cols], preferred_element_type=F32)
             rest = jnp.dot(a_high, s_low[:, cols], preferred_element_type=F32)
@@ -188,6 +271,8 @@
     def outside(phase, out, scale):
         for faces in ((2, 3), (0, 1)):
             for f in faces:
+                if f < 2 and phase not in WHOLE:
+                    continue
                 pl.when(comes[f])(face_copy(kept, STEPS + 1, phase, 0, f, f ^ 1).wait_recv)
             for f in faces:
                 ref = (halo_x, halo_x, halo_y, halo_y)[f]
@@ -227,12 +312,15 @@
     lifts = jnp.concatenate([lift[f] for f in range(6)], axis=0).T
     a_high, a_low = halves(jnp.concatenate([weight, lifts], axis=1))
     a_both = jnp.concatenate([a_high, a_low], axis=0)
-    face_matrix = []
+    thirds = []
     for f in range(4):
         high, low = halves(lifts[:, 16 * f : 16 * f + 16])
-        face_matrix.append(
-            jnp.concatenate([high.astype(F32), high.astype(F32), low.astype(F32)], axis=1).astype(BF16)
-        )
+        thirds.append(jnp.concatenate([high.astype(F32), high.astype(F32), low.astype(F32)], axis=1))
+    face_matrix = [third.astype(BF16) for third in thirds]
+    edge_matrix = []
+    for fx, low in ((0, 48), (1, 0)):
+        rows = [thirds[f][low : low + 16] for f in (1 - fx, 2, 3)]
+        edge_matrix.append(jnp.concatenate(rows, axis=1).astype(BF16))
 
     @pl.when(jnp.logical_not(first))
     def _():
@@ -251,7 +339,11 @@
             value = now[cell] + delta + source[cell]
             out[cell] = value - kept[cell] if last else value
 
-        inside(now, finish)
+        if step in PAIRED:
+            inside(now, finish, functools.partial(send_edges, PAIRED.index(step), out))
+        else:
+            inside(now, finish)
+            next_faces(step - 1)
         outside(step, out, 1.0)
 
     def err_copy(x):
@@ -290,6 +382,9 @@
 
     for step in range(1, STEPS):
         sent_faces(fields.at[step], step, step, 0)
+    for pair in range(len(PAIRED)):
+        for f in range(2):
+            pl.when(exists[f])(edge_copy(pair, f).wait_send)
 
     @pl.when(more)
     def _():
@@ -342,6 +437,9 @@
                 pltpu.VMEM((STEPS + 1, 2, ny, 16, nz), F32),
                 pltpu.VMEM((STEPS + 1, 2, nx, 16, nz), F32),
                 pltpu.VMEM((STEPS + 2, 2, nx, 16, nz), F32),
+                pltpu.VMEM((STEPS // 2, 2, 2, 16, nz), F32),
+                pltpu.VMEM((STEPS // 2, 2, ny, 16, nz), F32),
+                pltpu.VMEM((STEPS // 2, 2, ny, 16, nz), F32),
                 stack, stack,
                 pltpu.SemaphoreType.DMA((5,)),
                 pltpu.SemaphoreType.DMA((STEPS + 2, 4)),
@@ -350,6 +448,10 @@
                 pltpu.SemaphoreType.DMA((nx,)),
                 pltpu.SemaphoreType.DMA((nx,)),
                 pltpu.SemaphoreType.DMA((nx,)),
+                pltpu.SemaphoreType.DMA((STEPS + 2, 4)),
+                pltpu.SemaphoreType.DMA((STEPS // 2, 4)),
+                pltpu.SemaphoreType.DMA((STEPS // 2, 2)),
+                pltpu.SemaphoreType.DMA((STEPS // 2, 2)),
             ],
             compiler_params=pltpu.CompilerParams(
                 collective_id=0, has_side_effects=True, vmem_limit_bytes=32 * 2**20

time: 24.6 us -> 26.2 us (1.065)
  Pallas kernels: 23.8 us -> 25.4 us
    pallas_call x1, Pallas kernels: 22.7 us -> 24.3 us  [local(): pl.pallas_call(functools.partial(kernel, counts, nx, ny), out_shape=(shap...]
where the time goes in v4:
time: 26.2 us; the launch traced here: 26.1 us
  Pallas kernels  25.4 us (97%)
  between operations  0.64 us (2%)
    pallas_call x1, Pallas kernels, local(): pl.pallas_call(functools.partial(kernel, counts, nx, ny), out_shape=(shap...  24.3 us
    pallas_call x1, Pallas kernels, local(): pl.pallas_call(functools.partial(finishing, nx, ny), out_shape=(flat,) *...  1.08 us

profile of v4, /device:TPU:1, one launch (start us, length us, event | category | flops | bytes accessed | tf_op | source)
XLA Modules:
  0.0 26.1 jit_solution(2899136079159323288)
XLA Ops:
  0.6 24.3 %cycle.1 = (f32[16,64,128]{2,1,0:T(8,128)S(1)}, f32[16,64,128]{2,1,0:T(8,128)S(1)}, f32[16,64,128]{2,1,0:T(8,128)S(1)}) custom-call(f32[1024,128]{1,0:T(8,128)} %bitcast.6, f32[1024,128]{1,0:T(8,128)} %bitcast.7, f32[1024,128]{1,0:T(8,128)} %bitcast.8, f32[64,64]{1,0:T(8,128)} %vol_hbm.1, f32[6,16,64]{2,1,0:T(8,128)} %bitcast.9), custom_call_target="tpu_custom_call" | custom-call | tf_op jit(solution)/shard_map/cycle/pallas_call | solution.py:429
  25.0 1.1 %finishing.1 = (f32[1024,128]{1,0:T(8,128)}, f32[1024,128]{1,0:T(8,128)}) custom-call(f32[16,64,128]{2,1,0:T(8,128)S(1)} %get-tuple-element.7.kept, f32[16,64,128]{2,1,0:T(8,128)S(1)} %get-tuple-element.8.resid, f32[16,64,128]{2,1,0:T(8,128)S(1)} %get-tuple-element.9.error), custom_call_target="tpu_custom_call" | custom-call | tf_op jit(solution)/shard_map/finishing/pallas_call | solution.py:469

commit v5 on v3

--- a/solution.py
+++ b/solution.py
@@ -23,7 +23,7 @@
     state_hbm, force_hbm, init_hbm, vol_hbm, lift_hbm,
     kept, resid, error,
     raw_start, raw_state, raw_force, volume, lift,
-    fields, source, earlier,
+    fields, added,
     halo_x, halo_y, sent_y, s_high, s_low,
     load_sem, face_send, face_recv, start_send, start_recv, err_send, err_recv,
 ):
@@ -194,20 +194,17 @@
                 count = ref.shape[2]
                 trace = jnp.concatenate([ref[phase, f % 2, i] for i in range(count)], axis=1)
                 high, low = halves(trace)
-                added = jnp.dot(
+                more_delta = scale * jnp.dot(
                     face_matrix[f], jnp.concatenate([high, low, high], axis=0), preferred_element_type=F32
                 )
-                if scale != 1.0:
-                    added = scale * added
                 for i in range(count):
                     cell = (i, cells - ny + i, i * ny, i * ny + ny - 1)[f]
-                    out[cell] = out[cell] + added[:, i * LANES : (i + 1) * LANES]
+                    out[cell] = out[cell] + more_delta[:, i * LANES : (i + 1) * LANES]
 
     @pl.when(first)
     def _():
         load_init.wait()
         reorder(raw_start, fields.at[0])
-        send_faces(fields.at[0], 0, 0, 0)
 
     load_state.wait()
     reorder(raw_state, kept)
@@ -217,7 +214,7 @@
         send_faces(kept, STEPS + 1, 0, 1)
 
     load_force.wait()
-    reorder(raw_force, source)
+    reorder(raw_force, added.at[0])
 
     load_volume.wait()
     load_lift.wait()
@@ -240,56 +237,66 @@
             start_copy(x).wait_recv()
         reorder(raw_start, fields.at[0])
 
-    for step in range(STEPS):
-        now = fields.at[step]
-        last = step == STEPS - 1
-        out = resid if last else fields.at[step + 1]
-        if step > 0:
-            send_faces(now, step, step, 0)
-
-        def finish(cell, delta, now=now, out=out, last=last):
-            value = now[cell] + delta + source[cell]
-            out[cell] = value - kept[cell] if last else value
-
-        inside(now, finish)
-        outside(step, out, 1.0)
-
     def err_copy(x):
         part = pl.ds(x * ny, ny)
         return pltpu.make_async_remote_copy(
-            src_ref=error.at[part], dst_ref=earlier.at[part],
+            src_ref=fields.at[STEPS + 2, part], dst_ref=fields.at[STEPS + 1, part],
             send_sem=err_send.at[x], recv_sem=err_recv.at[x],
             device_id={"tm": tm + 1, "sx": sx, "sy": sy}, device_id_type=MESH,
         )
 
+    def advance(turn, _):
+        coarse = turn == STEPS
+        place_in = turn + coarse.astype(jnp.int32)
+        now, out = fields.at[place_in], fields.at[place_in + 1]
+        adding = added.at[coarse.astype(jnp.int32)]
+        scale = jnp.where(coarse, 4.0, 1.0).astype(F32)
+
+        @pl.when(((turn > 0) | first) & (turn < STEPS))
+        def _():
+            send_faces(now, turn, turn, 0)
+
+        @pl.when(coarse)
+        def _():
+            for x in range(nx):
+                err_copy(x).wait_recv()
+
+        def finish(cell, delta):
+            out[cell] = now[cell] + scale * delta + adding[cell]
+
+        inside(now, finish)
+        outside(turn, out, scale)
+
+        @pl.when(turn == STEPS - 1)
+        def _():
+            for cell in range(cells):
+                value = fields[STEPS, cell] - kept[cell]
+                resid[cell] = value
+                added[1, cell] = value
+                fields[STEPS + 2, cell] = value
+
+        return 0
+
+    lax.fori_loop(0, jnp.where(first, STEPS, STEPS + 1), advance, 0)
+
+    @pl.when(more)
+    def _():
+        send_faces(fields.at[STEPS + 2], STEPS, STEPS, 1)
+        for x in range(nx):
+            err_copy(x).start()
+
+    for cell in range(cells):
+        error[cell] = fields[STEPS + 2, cell]
+
     @pl.when(first)
     def _():
-        for cell in range(cells):
-            error[cell] = resid[cell]
-
-    @pl.when(jnp.logical_not(first))
-    def _():
-        for x in range(nx):
-            err_copy(x).wait_recv()
-
-        def finish(cell, delta):
-            error[cell] = resid[cell] + earlier[cell] + 4.0 * delta
-
-        inside(earlier, finish)
-        outside(STEPS, error, 4.0)
-
-    @pl.when(more)
-    def _():
-        send_faces(error, STEPS, STEPS, 1)
-        for x in range(nx):
-            err_copy(x).start()
-
-    @pl.when(first)
-    def _():
         sent_faces(fields.at[0], 0, 0, 0)
 
-    for step in range(1, STEPS):
-        sent_faces(fields.at[step], step, step, 0)
+    def sent_turn(turn, _):
+        sent_faces(fields.at[turn], turn, turn, 0)
+        return 0
+
+    lax.fori_loop(1, STEPS, sent_turn, 0)
 
     @pl.when(more)
     def _():
@@ -297,7 +304,7 @@
         for x in range(nx):
             start_copy(x).wait_send()
             err_copy(x).wait_send()
-        sent_faces(error, STEPS, STEPS, 1)
+        sent_faces(fields.at[STEPS + 2], STEPS, STEPS, 1)
 
 
 def finishing(nx, ny, kept, resid, error, corr_hbm, resid_hbm, out_c, out_r, out_sem):
@@ -326,7 +333,6 @@
         cells = nx * ny
         rows = dofs * cells
         raw = pltpu.VMEM((rows, nz), F32)
-        field = pltpu.VMEM((cells, dofs, nz), F32)
         stack = pltpu.VMEM((160, cells * nz), BF16)
         flat = jax.ShapeDtypeStruct((rows, nz), F32)
         shaped = jax.ShapeDtypeStruct((cells, dofs, nz), F32)
@@ -338,7 +344,7 @@
             out_specs=(vmem,) * 3,
             scratch_shapes=[
                 raw, raw, raw, pltpu.VMEM(volume.shape, F32), pltpu.VMEM((6, 16, dofs), F32),
-                pltpu.VMEM((STEPS, cells, dofs, nz), F32), field, field,
+                pltpu.VMEM((STEPS + 3, cells, dofs, nz), F32), pltpu.VMEM((2, cells, dofs, nz), F32),
                 pltpu.VMEM((STEPS + 1, 2, ny, 16, nz), F32),
                 pltpu.VMEM((STEPS + 1, 2, nx, 16, nz), F32),
                 pltpu.VMEM((STEPS + 2, 2, nx, 16, nz), F32),

time: 24.6 us -> 25.6 us (1.041)
  Pallas kernels: 23.8 us -> 24.8 us
    pallas_call x1, Pallas kernels: 22.7 us -> 23.7 us  [local(): pl.pallas_call(functools.partial(kernel, counts, nx, ny), out_shape=(shap...]
where the time goes in v5:
time: 25.6 us; the launch traced here: 25.4 us
  Pallas kernels  24.8 us (97%)
  between operations  0.64 us (2%)
    pallas_call x1, Pallas kernels, local(): pl.pallas_call(functools.partial(kernel, counts, nx, ny), out_shape=(shap...  23.7 us
    pallas_call x1, Pallas kernels, local(): pl.pallas_call(functools.partial(finishing, nx, ny), out_shape=(flat,) *...  1.08 us

profile of v5, /device:TPU:1, one launch (start us, length us, event | category | flops | bytes accessed | tf_op | source)
XLA Modules:
  0.0 25.4 jit_solution(14424232951063724106)
XLA Ops:
  0.6 23.7 %cycle.1 = (f32[16,64,128]{2,1,0:T(8,128)S(1)}, f32[16,64,128]{2,1,0:T(8,128)S(1)}, f32[16,64,128]{2,1,0:T(8,128)S(1)}) custom-call(f32[1024,128]{1,0:T(8,128)} %bitcast.6, f32[1024,128]{1,0:T(8,128)} %bitcast.7, f32[1024,128]{1,0:T(8,128)} %bitcast.8, f32[64,64]{1,0:T(8,128)} %vol_hbm.1, f32[6,16,64]{2,1,0:T(8,128)} %bitcast.9), custom_call_target="tpu_custom_call" | custom-call | tf_op jit(solution)/shard_map/cycle/pallas_call | solution.py:340
  24.4 1.1 %finishing.1 = (f32[1024,128]{1,0:T(8,128)}, f32[1024,128]{1,0:T(8,128)}) custom-call(f32[16,64,128]{2,1,0:T(8,128)S(1)} %get-tuple-element.7.kept, f32[16,64,128]{2,1,0:T(8,128)S(1)} %get-tuple-element.8.resid, f32[16,64,128]{2,1,0:T(8,128)S(1)} %get-tuple-element.9.error), custom_call_target="tpu_custom_call" | custom-call | tf_op jit(solution)/shard_map/finishing/pallas_call | solution.py:373

commit v6 on v2

--- a/solution.py
+++ b/solution.py
@@ -24,7 +24,7 @@
     kept, resid, error,
     raw_start, raw_state, raw_force, volume, lift,
     fields, source, earlier,
-    halo_x, halo_y, sent_y, s_high, s_low,
+    halo_x, halo_y, sent_y, stack, lows,
     load_sem, face_send, face_recv, start_send, start_recv, err_send, err_recv,
 ):
     n_tm, n_sx, n_sy = counts
@@ -70,13 +70,13 @@
         )
 
     wide, tall = ny * LANES, cells * LANES
-    for stack in (s_high, s_low):
-        stack[64:80, 0:wide] = jnp.zeros((16, wide), BF16)
-        stack[80:96, tall - wide : tall] = jnp.zeros((16, wide), BF16)
-        for x in range(nx):
-            low, high = x * wide, (x + 1) * wide
-            stack[96:112, low : low + LANES] = jnp.zeros((16, LANES), BF16)
-            stack[112:128, high - LANES : high] = jnp.zeros((16, LANES), BF16)
+    for shift in (0, 96):
+        stack[64 + shift : 80 + shift, 0:wide] = jnp.zeros((16, wide), BF16)
+        stack[80 + shift : 96 + shift, tall - wide : tall] = jnp.zeros((16, wide), BF16)
+        for x in range(nx):
+            left, right = x * wide, (x + 1) * wide
+            stack[96 + shift : 112 + shift, left : left + LANES] = jnp.zeros((16, LANES), BF16)
+            stack[112 + shift : 128 + shift, right - LANES : right] = jnp.zeros((16, LANES), BF16)
 
     def no_halo(f):
         ref = (halo_x, halo_x, halo_y, halo_y)[f]
@@ -134,8 +134,10 @@
         )
 
     def send_faces(ref, slot, phase, dt):
-        for f in range(2):
-            pl.when(exists[f])(face_copy(ref, slot, phase, dt, f).start)
+        odd = lax.rem(sx, 2) == 1
+        pl.when(exists[0] & odd)(face_copy(ref, slot, phase, dt, 0).start)
+        pl.when(exists[1])(face_copy(ref, slot, phase, dt, 1).start)
+        pl.when(exists[0] & jnp.logical_not(odd))(face_copy(ref, slot, phase, dt, 0).start)
         for x in range(nx):
             sent_y[slot, 0, x] = y_plus(ref, x * ny + ny - 1)
             sent_y[slot, 1, x] = y_minus(ref, x * ny)
@@ -151,54 +153,60 @@
             ref[cell] = raw[pl.ds(cell, 64, stride=cells), :]
 
     def inside(ref, finish):
-        def put(rows, cell, value):
-            high, low = halves(value)
+        def put(rows, cell, pair):
             cols = slice(cell * LANES, (cell + 1) * LANES)
-            s_high[rows : rows + value.shape[0], cols] = high
-            s_low[rows : rows + value.shape[0], cols] = low
+            stack[rows : rows + 16, cols] = pair[0]
+            stack[rows + 96 : rows + 112, cols] = pair[1]
 
         for x in range(nx):
             for y in range(ny):
                 cell = x * ny + y
-                pair = halves(ref[cell])
-                for stack, half in zip((s_high, s_low), pair):
-                    stack[0:64, cell * LANES : (cell + 1) * LANES] = half
-                    if x + 1 < nx:
-                        stack[64:80, (cell + ny) * LANES : (cell + ny + 1) * LANES] = half[48:64]
-                    if x > 0:
-                        stack[80:96, (cell - ny) * LANES : (cell - ny + 1) * LANES] = half[0:16]
+                high, low = halves(ref[cell])
+                stack[0:64, cell * LANES : (cell + 1) * LANES] = high
+                lows[x * 64 : (x + 1) * 64, y * LANES : (y + 1) * LANES] = low
+                if x + 1 < nx:
+                    put(64, cell + ny, (high[48:64], low[48:64]))
+                if x > 0:
+                    put(80, cell - ny, (high[0:16], low[0:16]))
                 if y + 1 < ny:
-                    put(96, cell + 1, y_plus(ref, cell))
+                    put(96, cell + 1, halves(y_plus(ref, cell)))
                 if y > 0:
-                    put(112, cell - 1, y_minus(ref, cell))
+                    put(112, cell - 1, halves(y_minus(ref, cell)))
                 up = pltpu.roll(ref[cell, pl.ds(3, 16, stride=4), :], 1, 1)
-                put(128, cell, jnp.where(lane == 0, 0.0, up))
+                put(128, cell, halves(jnp.where(lane == 0, 0.0, up)))
                 down = pltpu.roll(ref[cell, pl.ds(0, 16, stride=4), :], LANES - 1, 1)
-                put(144, cell, jnp.where(lane == LANES - 1, 0.0, down))
+                put(144, cell, halves(jnp.where(lane == LANES - 1, 0.0, down)))
+        rest = jnp.dot(low_matrix, lows[...], preferred_element_type=F32)
         for x in range(nx):
             cols = slice(x * wide, (x + 1) * wide)
-            both = jnp.dot(a_both, s_high[:, cols], preferred_element_type=F32)
-            rest = jnp.dot(a_high, s_low[:, cols], preferred_element_type=F32)
-            delta = both[:64] + both[64:] + rest
+            both = jnp.dot(main_matrix, stack[:, cols], preferred_element_type=F32)
+            delta = both[:64] + both[64:] + rest[x * 64 : (x + 1) * 64]
             for y in range(ny):
                 finish(x * ny + y, delta[:, y * LANES : (y + 1) * LANES])
 
     def outside(phase, out, scale):
         for f in range(4):
             pl.when(comes[f])(face_copy(kept, STEPS + 1, phase, 0, f, f ^ 1).wait_recv)
+        rows = []
         for f in range(4):
             ref = (halo_x, halo_x, halo_y, halo_y)[f]
-            count = ref.shape[2]
-            trace = jnp.concatenate([ref[phase, f % 2, i] for i in range(count)], axis=1)
-            high, low = halves(trace)
-            added = jnp.dot(
-                face_matrix[f], jnp.concatenate([high, low, high], axis=0), preferred_element_type=F32
-            )
-            if scale != 1.0:
-                added = scale * added
-            for i in range(count):
+            blocks = [ref[phase, f % 2, i] for i in range(ref.shape[2])]
+            blocks += [jnp.zeros((16, LANES), F32)] * (max(nx, ny) - len(blocks))
+            high, low = halves(jnp.concatenate(blocks, axis=1))
+            rows += [high, low, high]
+        more_delta = jnp.dot(
+            face_matrix, jnp.concatenate(rows, axis=0), preferred_element_type=F32
+        )
+        if scale != 1.0:
+            more_delta = scale * more_delta
+        sums = {}
+        for f in range(4):
+            for i in range((ny, ny, nx, nx)[f]):
                 cell = (i, cells - ny + i, i * ny, i * ny + ny - 1)[f]
-                out[cell] = out[cell] + added[:, i * LANES : (i + 1) * LANES]
+                part = more_delta[f * 64 : (f + 1) * 64, i * LANES : (i + 1) * LANES]
+                sums[cell] = sums[cell] + part if cell in sums else part
+        for cell, part in sums.items():
+            out[cell] = out[cell] + part
 
     @pl.when(first)
     def _():
@@ -222,14 +230,32 @@
     column = lax.broadcasted_iota(jnp.int32, (64, 64), 1)
     weight = volume[...] - jnp.where(row == column, 0.1, 0.0).astype(F32)
     lifts = jnp.concatenate([lift[f] for f in range(6)], axis=0).T
-    a_high, a_low = halves(jnp.concatenate([weight, lifts], axis=1))
-    a_both = jnp.concatenate([a_high, a_low], axis=0)
-    face_matrix = []
-    for f in range(4):
-        high, low = halves(lifts[:, 16 * f : 16 * f + 16])
-        face_matrix.append(
-            jnp.concatenate([high.astype(F32), high.astype(F32), low.astype(F32)], axis=1).astype(BF16)
-        )
+    high, low = (half.astype(F32) for half in halves(jnp.concatenate([weight, lifts], axis=1)))
+
+    def diagonal(blocks):
+        rows, cols = blocks[0].shape
+        return jnp.concatenate(
+            [
+                jnp.concatenate(
+                    [block if i == j else jnp.zeros((rows, cols), F32) for j in range(len(blocks))], axis=1
+                )
+                for i, block in enumerate(blocks)
+            ],
+            axis=0,
+        ).astype(BF16)
+
+    main_matrix = jnp.concatenate(
+        [
+            jnp.concatenate([high, high[:, 64:]], axis=1),
+            jnp.concatenate([low, jnp.zeros((64, 96), F32)], axis=1),
+        ],
+        axis=0,
+    ).astype(BF16)
+    low_matrix = diagonal([high[:, :64]] * nx)
+    faces = [slice(64 + 16 * f, 80 + 16 * f) for f in range(4)]
+    face_matrix = diagonal(
+        [jnp.concatenate([high[:, at], high[:, at], low[:, at]], axis=1) for at in faces]
+    )
 
     @pl.when(jnp.logical_not(first))
     def _():
@@ -277,9 +303,9 @@
 
     @pl.when(more)
     def _():
+        send_faces(error, STEPS, STEPS, 1)
         for x in range(nx):
             err_copy(x).start()
-        send_faces(error, STEPS, STEPS, 1)
 
     @pl.when(first)
     def _():
@@ -324,7 +350,6 @@
         rows = dofs * cells
         raw = pltpu.VMEM((rows, nz), F32)
         field = pltpu.VMEM((cells, dofs, nz), F32)
-        stack = pltpu.VMEM((160, cells * nz), BF16)
         flat = jax.ShapeDtypeStruct((rows, nz), F32)
         shaped = jax.ShapeDtypeStruct((cells, dofs, nz), F32)
         vmem, hbm = pl.BlockSpec(memory_space=pltpu.VMEM), pl.BlockSpec(memory_space=pltpu.HBM)
@@ -339,7 +364,7 @@
                 pltpu.VMEM((STEPS + 1, 2, ny, 16, nz), F32),
                 pltpu.VMEM((STEPS + 1, 2, nx, 16, nz), F32),
                 pltpu.VMEM((STEPS + 2, 2, nx, 16, nz), F32),
-                stack, stack,
+                pltpu.VMEM((256, cells * nz), BF16), pltpu.VMEM((dofs * nx, ny * nz), BF16),
                 pltpu.SemaphoreType.DMA((5,)),
                 pltpu.SemaphoreType.DMA((STEPS + 2, 4)),
                 pltpu.SemaphoreType.DMA((STEPS + 1, 4)),

time: 24.6 us -> 24.3 us (0.988)
    pallas_call x1, Pallas kernels: 22.8 us -> 22.5 us  [local(): pl.pallas_call(functools.partial(kernel, counts, nx, ny), out_shape=(shap...]
where the time goes in v6:
time: 24.3 us; the launch traced here: 24.2 us
  Pallas kernels  23.6 us (97%)
  between operations  0.64 us (3%)
    pallas_call x1, Pallas kernels, local(): pl.pallas_call(functools.partial(kernel, counts, nx, ny), out_shape=(shap...  22.5 us
    pallas_call x1, Pallas kernels, local(): pl.pallas_call(functools.partial(finishing, nx, ny), out_shape=(flat,) *...  1.08 us

profile of v6, /device:TPU:1, one launch (start us, length us, event | category | flops | bytes accessed | tf_op | source)
XLA Modules:
  0.0 24.2 jit_solution(13830974143515329185)
XLA Ops:
  0.6 22.5 %cycle.1 = (f32[16,64,128]{2,1,0:T(8,128)S(1)}, f32[16,64,128]{2,1,0:T(8,128)S(1)}, f32[16,64,128]{2,1,0:T(8,128)S(1)}) custom-call(f32[1024,128]{1,0:T(8,128)} %bitcast.6, f32[1024,128]{1,0:T(8,128)} %bitcast.7, f32[1024,128]{1,0:T(8,128)} %bitcast.8, f32[64,64]{1,0:T(8,128)} %vol_hbm.1, f32[6,16,64]{2,1,0:T(8,128)} %bitcast.9), custom_call_target="tpu_custom_call" | custom-call | tf_op jit(solution)/shard_map/cycle/pallas_call | solution.py:356
  23.1 1.1 %finishing.1 = (f32[1024,128]{1,0:T(8,128)}, f32[1024,128]{1,0:T(8,128)}) custom-call(f32[16,64,128]{2,1,0:T(8,128)S(1)} %get-tuple-element.7.kept, f32[16,64,128]{2,1,0:T(8,128)S(1)} %get-tuple-element.8.resid, f32[16,64,128]{2,1,0:T(8,128)S(1)} %get-tuple-element.9.error), custom_call_target="tpu_custom_call" | custom-call | tf_op jit(solution)/shard_map/finishing/pallas_call | solution.py:389

commit v7 on v6

--- a/solution.py
+++ b/solution.py
@@ -39,6 +39,21 @@
         dx, dy = shifts[f]
         return {"tm": tm + dt, "sx": sx + dx, "sy": sy + dy}
 
+    barrier = pltpu.get_barrier_semaphore()
+
+    def greet(dt, f):
+        pl.semaphore_signal(barrier, inc=1, device_id=place(dt, f), device_id_type=MESH)
+
+    for f in range(4):
+        pl.when(exists[f])(functools.partial(greet, 0, f))
+        pl.when(exists[f] & (tm > 0))(functools.partial(greet, -1, f))
+
+    @pl.when(tm > 0)
+    def _():
+        pl.semaphore_signal(
+            barrier, inc=1, device_id={"tm": tm - 1, "sx": sx, "sy": sy}, device_id_type=MESH
+        )
+
     load_state = pltpu.make_async_copy(state_hbm, raw_state, load_sem.at[0])
     load_force = pltpu.make_async_copy(force_hbm, raw_force, load_sem.at[1])
     load_init = pltpu.make_async_copy(init_hbm, raw_start, load_sem.at[2])
@@ -53,21 +68,6 @@
     load_lift = pltpu.make_async_copy(lift_hbm, lift, load_sem.at[4])
     load_volume.start()
     load_lift.start()
-
-    barrier = pltpu.get_barrier_semaphore()
-
-    def greet(dt, f):
-        pl.semaphore_signal(barrier, inc=1, device_id=place(dt, f), device_id_type=MESH)
-
-    for f in range(4):
-        pl.when(exists[f])(functools.partial(greet, 0, f))
-        pl.when(exists[f] & (tm > 0))(functools.partial(greet, -1, f))
-
-    @pl.when(tm > 0)
-    def _():
-        pl.semaphore_signal(
-            barrier, inc=1, device_id={"tm": tm - 1, "sx": sx, "sy": sy}, device_id_type=MESH
-        )
 
     wide, tall = ny * LANES, cells * LANES
     for shift in (0, 96):
@@ -129,7 +129,7 @@
         target = (halo_x, halo_x, halo_y, halo_y)[f].at[phase, f % 2]
         return pltpu.make_async_remote_copy(
             src_ref=src, dst_ref=target,
-            send_sem=face_send.at[slot, f], recv_sem=face_recv.at[phase, f],
+            send_sem=face_send.at[dt, f], recv_sem=face_recv.at[phase, f],
             device_id=place(dt, f if to is None else to), device_id_type=MESH,
         )
 
@@ -144,9 +144,14 @@
         for f in range(2, 4):
             pl.when(exists[f])(face_copy(ref, slot, phase, dt, f).start)
 
-    def sent_faces(ref, slot, phase, dt):
+    def sent_faces(dt, phases):
         for f in range(4):
-            pl.when(exists[f])(face_copy(ref, slot, phase, dt, f).wait_send)
+            block = (halo_x, halo_x, halo_y, halo_y)[f].at[pl.ds(0, phases), f % 2]
+            copy = pltpu.make_async_remote_copy(
+                src_ref=block, dst_ref=block, send_sem=face_send.at[dt, f], recv_sem=face_recv.at[0, f],
+                device_id=place(dt, f), device_id_type=MESH,
+            )
+            pl.when(exists[f])(copy.wait_send)
 
     def reorder(raw, ref):
         for cell in range(cells):
@@ -263,6 +268,32 @@
             start_copy(x).wait_recv()
         reorder(raw_start, fields.at[0])
 
+    early = [(x * ny + 1, ny - 2) for x in range(1, nx - 1)] if ny > 2 else []
+    marks = [0] + [edge for start, size in early for edge in (start, start + size)] + [cells]
+    late = [(low, high - low) for low, high in zip(marks[::2], marks[1::2])]
+
+    def err_copy(part, ref):
+        at = pl.ds(*part)
+        index = (early + late).index(part)
+        return pltpu.make_async_remote_copy(
+            src_ref=ref.at[at], dst_ref=earlier.at[at],
+            send_sem=err_send.at[index], recv_sem=err_recv.at[index],
+            device_id={"tm": tm + 1, "sx": sx, "sy": sy}, device_id_type=MESH,
+        )
+
+    def send_early(ref):
+        @pl.when(more)
+        def _():
+            for part in early:
+                err_copy(part, ref).start()
+
+    def send_late(ref):
+        @pl.when(more)
+        def _():
+            send_faces(ref, STEPS, STEPS, 1)
+            for part in late:
+                err_copy(part, ref).start()
+
     for step in range(STEPS):
         now = fields.at[step]
         last = step == STEPS - 1
@@ -275,52 +306,38 @@
             out[cell] = value - kept[cell] if last else value
 
         inside(now, finish)
+        if last:
+            pl.when(first)(functools.partial(send_early, resid))
         outside(step, out, 1.0)
 
-    def err_copy(x):
-        part = pl.ds(x * ny, ny)
-        return pltpu.make_async_remote_copy(
-            src_ref=error.at[part], dst_ref=earlier.at[part],
-            send_sem=err_send.at[x], recv_sem=err_recv.at[x],
-            device_id={"tm": tm + 1, "sx": sx, "sy": sy}, device_id_type=MESH,
-        )
-
     @pl.when(first)
     def _():
+        send_late(resid)
         for cell in range(cells):
             error[cell] = resid[cell]
+        sent_faces(0, STEPS)
 
     @pl.when(jnp.logical_not(first))
     def _():
-        for x in range(nx):
-            err_copy(x).wait_recv()
+        sent_faces(0, STEPS - 1)
+        for part in early + late:
+            err_copy(part, error).wait_recv()
 
         def finish(cell, delta):
             error[cell] = resid[cell] + earlier[cell] + 4.0 * delta
 
         inside(earlier, finish)
+        send_early(error)
         outside(STEPS, error, 4.0)
+        send_late(error)
 
     @pl.when(more)
     def _():
-        send_faces(error, STEPS, STEPS, 1)
-        for x in range(nx):
-            err_copy(x).start()
-
-    @pl.when(first)
-    def _():
-        sent_faces(fields.at[0], 0, 0, 0)
-
-    for step in range(1, STEPS):
-        sent_faces(fields.at[step], step, step, 0)
-
-    @pl.when(more)
-    def _():
-        sent_faces(kept, STEPS + 1, 0, 1)
         for x in range(nx):
             start_copy(x).wait_send()
-            err_copy(x).wait_send()
-        sent_faces(error, STEPS, STEPS, 1)
+        for part in early + late:
+            err_copy(part, resid).wait_send()
+        sent_faces(1, 2)
 
 
 def finishing(nx, ny, kept, resid, error, corr_hbm, resid_hbm, out_c, out_r, out_sem):
@@ -366,12 +383,12 @@
                 pltpu.VMEM((STEPS + 2, 2, nx, 16, nz), F32),
                 pltpu.VMEM((256, cells * nz), BF16), pltpu.VMEM((dofs * nx, ny * nz), BF16),
                 pltpu.SemaphoreType.DMA((5,)),
-                pltpu.SemaphoreType.DMA((STEPS + 2, 4)),
+                pltpu.SemaphoreType.DMA((2, 4)),
                 pltpu.SemaphoreType.DMA((STEPS + 1, 4)),
                 pltpu.SemaphoreType.DMA((nx,)),
                 pltpu.SemaphoreType.DMA((nx,)),
-                pltpu.SemaphoreType.DMA((nx,)),
-                pltpu.SemaphoreType.DMA((nx,)),
+                pltpu.SemaphoreType.DMA((2 * nx,)),
+                pltpu.SemaphoreType.DMA((2 * nx,)),
             ],
             compiler_params=pltpu.CompilerParams(
                 collective_id=0, has_side_effects=True, vmem_limit_bytes=32 * 2**20

time: 24.3 us -> 24.2 us (level)
  no operation moved by 1% of the time
where the time goes in v7:
time: 24.2 us; the launch traced here: 24.1 us
  Pallas kernels  23.4 us (97%)
  between operations  0.64 us (3%)
    pallas_call x1, Pallas kernels, local(): pl.pallas_call(functools.partial(kernel, counts, nx, ny), out_shape=(shap...  22.3 us
    pallas_call x1, Pallas kernels, local(): pl.pallas_call(functools.partial(finishing, nx, ny), out_shape=(flat,) *...  1.08 us

profile of v7, /device:TPU:1, one launch (start us, length us, event | category | flops | bytes accessed | tf_op | source)
XLA Modules:
  0.0 24.1 jit_solution(7680265675455327195)
XLA Ops:
  0.6 22.3 %cycle.1 = (f32[16,64,128]{2,1,0:T(8,128)S(1)}, f32[16,64,128]{2,1,0:T(8,128)S(1)}, f32[16,64,128]{2,1,0:T(8,128)S(1)}) custom-call(f32[1024,128]{1,0:T(8,128)} %bitcast.6, f32[1024,128]{1,0:T(8,128)} %bitcast.7, f32[1024,128]{1,0:T(8,128)} %bitcast.8, f32[64,64]{1,0:T(8,128)} %vol_hbm.1, f32[6,16,64]{2,1,0:T(8,128)} %bitcast.9), custom_call_target="tpu_custom_call" | custom-call | tf_op jit(solution)/shard_map/cycle/pallas_call | solution.py:373
  23.0 1.1 %finishing.1 = (f32[1024,128]{1,0:T(8,128)}, f32[1024,128]{1,0:T(8,128)}) custom-call(f32[16,64,128]{2,1,0:T(8,128)S(1)} %get-tuple-element.7.kept, f32[16,64,128]{2,1,0:T(8,128)S(1)} %get-tuple-element.8.resid, f32[16,64,128]{2,1,0:T(8,128)S(1)} %get-tuple-element.9.error), custom_call_target="tpu_custom_call" | custom-call | tf_op jit(solution)/shard_map/finishing/pallas_call | solution.py:406

commit v8 on v4

--- a/solution.py
+++ b/solution.py
@@ -26,7 +26,7 @@
     kept, resid, error,
     raw_start, raw_state, raw_force, volume, lift,
     fields, source, earlier,
-    halo_x, halo_y, sent_y, corner, edge, sent_edge, s_high, s_low,
+    halo_x, halo_y, sent_y, corner, edge, sent_edge, edge_y, sent_edge_y, s_high, s_low,
     load_sem, face_send, face_recv, start_send, start_recv, err_send, err_recv,
     corner_send, corner_recv, edge_send, edge_recv,
 ):
@@ -105,7 +105,8 @@
 
     def no_corner(fx, fy):
         for pair in range(STEPS // 2):
-            corner[pair, fx, fy - 2] = jnp.zeros((16, LANES), F32)
+            for kind in range(2):
+                corner[kind, pair, fx, fy - 2] = jnp.zeros((16, LANES), F32)
 
     for fx, fy in diagonals:
         pl.when(jnp.logical_not(comes[fx] & comes[fy]))(functools.partial(no_corner, fx, fy))
@@ -171,29 +172,37 @@
             pl.when(exists[f])(face_copy(ref, slot, phase, dt, f).start)
         if phase in PAIRED:
             for fx, fy in diagonals:
-                pl.when(exists[fx] & exists[fy])(corner_copy(slot, phase, dt, fx, fy).start)
+                for kind in range(2):
+                    copy = corner_copy(ref, slot, phase, dt, fx, fy, kind)
+                    pl.when(exists[fx] & exists[fy])(copy.start)
 
     def sent_faces(ref, slot, phase, dt):
         for f in range(4) if phase in WHOLE else range(2, 4):
             pl.when(exists[f])(face_copy(ref, slot, phase, dt, f).wait_send)
         if phase in PAIRED:
             for fx, fy in diagonals:
-                pl.when(exists[fx] & exists[fy])(corner_copy(slot, phase, dt, fx, fy).wait_send)
-
-    def corner_copy(slot, phase, dt, fx, fy, back=False):
-        cell = nx - 1 if fx == 0 else 0
-        pair = PAIRED.index(phase)
+                for kind in range(2):
+                    copy = corner_copy(ref, slot, phase, dt, fx, fy, kind)
+                    pl.when(exists[fx] & exists[fy])(copy.wait_send)
+
+    def corner_copy(ref, slot, phase, dt, fx, fy, kind, back=False):
+        x, y = (nx - 1 if fx == 0 else 0), (ny - 1 if fy == 2 else 0)
+        pair, index = PAIRED.index(phase), 2 * fx + fy - 2
+        if kind == 0:
+            src = sent_y.at[slot, fy - 2, x]
+        else:
+            src = ref.at[x * ny + y, pl.ds(48 if fx == 0 else 0, 16), :]
         target = across(dt, fx ^ 1, fy ^ 1) if back else across(dt, fx, fy)
         return pltpu.make_async_remote_copy(
-            src_ref=sent_y.at[slot, fy - 2, cell], dst_ref=corner.at[pair, fx, fy - 2],
-            send_sem=corner_send.at[slot, 2 * fx + fy - 2],
-            recv_sem=corner_recv.at[pair, 2 * fx + fy - 2],
+            src_ref=src, dst_ref=corner.at[kind, pair, fx, fy - 2],
+            send_sem=corner_send.at[kind, slot, index], recv_sem=corner_recv.at[kind, pair, index],
             device_id=target, device_id_type=MESH,
         )
 
     def edge_copy(pair, f, to=None):
+        src, dst = ((sent_edge, edge), (sent_edge_y, edge_y))[f // 2]
         return pltpu.make_async_remote_copy(
-            src_ref=sent_edge.at[pair, f], dst_ref=edge.at[pair, f],
+            src_ref=src.at[pair, f % 2], dst_ref=dst.at[pair, f % 2],
             send_sem=edge_send.at[pair, f], recv_sem=edge_recv.at[pair, f],
             device_id=place(0, f if to is None else to), device_id_type=MESH,
         )
@@ -205,28 +214,48 @@
         for f in range(2):
             pl.when(exists[f])(edge_copy(pair, f).start)
 
+    def send_edges_y(pair, ref):
+        for x in range(nx):
+            sent_edge_y[pair, 0, x] = y_plus(ref, x * ny + ny - 1)
+            sent_edge_y[pair, 1, x] = y_minus(ref, x * ny)
+        for f in range(2, 4):
+            pl.when(exists[f])(edge_copy(pair, f).start)
+
     def next_faces(phase):
         pair, now = PAIRED.index(phase), fields.at[phase]
-        for fx in range(2):
-
-            @pl.when(comes[fx])
-            def _(fx=fx):
-                edge_copy(pair, fx, fx ^ 1).wait_recv()
-                for fy in (2, 3):
-                    back = corner_copy(0, phase, 0, fx, fy, True)
-                    pl.when(comes[fy])(back.wait_recv)
-                cell, low = (0, 0) if fx == 0 else (cells - ny, 48)
-                own = [now[cell + y, low : low + 16, :] for y in range(ny)]
-                none = [jnp.zeros((16, LANES), F32)] * (ny - 1)
+        for f in range(4):
+
+            @pl.when(comes[f])
+            def _(f=f):
+                edge_copy(pair, f, f ^ 1).wait_recv()
+                sides = (2, 3) if f < 2 else (0, 1)
+                found = []
+                for g in sides:
+                    fx, fy = (f, g) if f < 2 else (g, f)
+                    back = corner_copy(now, 0, phase, 0, fx, fy, f // 2, True)
+                    pl.when(comes[g])(back.wait_recv)
+                    found.append(corner[f // 2, pair, fx, fy - 2])
+                if f < 2:
+                    count, kept_edge, halo = ny, edge, halo_x
+                    cell, low = (0, 0) if f == 0 else (cells - ny, 48)
+                    own = [now[cell + y, low : low + 16, :] for y in range(ny)]
+                else:
+                    count, kept_edge, halo = nx, edge_y, halo_y
+                    own = [
+                        y_minus(now, x * ny) if f == 2 else y_plus(now, x * ny + ny - 1) for x in range(nx)
+                    ]
+                none = [jnp.zeros((16, LANES), F32)] * (count - 1)
                 rows = []
-                for blocks in (own, [corner[pair, fx, 0]] + none, none + [corner[pair, fx, 1]]):
+                for blocks in (own, [found[0]] + none, none + [found[1]]):
                     high, part = halves(jnp.concatenate(blocks, axis=1))
                     rows += [high, part, high]
                 added = jnp.dot(
-                    edge_matrix[fx], jnp.concatenate(rows, axis=0), preferred_element_type=F32
+                    edge_matrix[f], jnp.concatenate(rows, axis=0), preferred_element_type=F32
                 )
-                for y in range(ny):
-                    halo_x[phase + 1, fx, y] = edge[pair, fx, y] + added[:, y * LANES : (y + 1) * LANES]
+                for i in range(count):
+                    halo[phase + 1, f % 2, i] = (
+                        kept_edge[pair, f % 2, i] + added[:, i * LANES : (i + 1) * LANES]
+                    )
 
     def reorder(raw, ref):
         for cell in range(cells):
@@ -271,7 +300,7 @@
     def outside(phase, out, scale):
         for faces in ((2, 3), (0, 1)):
             for f in faces:
-                if f < 2 and phase not in WHOLE:
+                if phase not in WHOLE:
                     continue
                 pl.when(comes[f])(face_copy(kept, STEPS + 1, phase, 0, f, f ^ 1).wait_recv)
             for f in faces:
@@ -318,9 +347,16 @@
         thirds.append(jnp.concatenate([high.astype(F32), high.astype(F32), low.astype(F32)], axis=1))
     face_matrix = [third.astype(BF16) for third in thirds]
     edge_matrix = []
-    for fx, low in ((0, 48), (1, 0)):
-        rows = [thirds[f][low : low + 16] for f in (1 - fx, 2, 3)]
-        edge_matrix.append(jnp.concatenate(rows, axis=1).astype(BF16))
+    for f in range(4):
+        picked = []
+        for g in (f ^ 1,) + ((2, 3) if f < 2 else (0, 1)):
+            third = thirds[g]
+            if f < 2:
+                picked.append(third[48:64] if f == 0 else third[0:16])
+            else:
+                low = 12 if f == 2 else 0
+                picked.append(jnp.concatenate([third[p + low : p + low + 4] for p in range(0, 64, 16)], axis=0))
+        edge_matrix.append(jnp.concatenate(picked, axis=1).astype(BF16))
 
     @pl.when(jnp.logical_not(first))
     def _():
@@ -332,7 +368,7 @@
         now = fields.at[step]
         last = step == STEPS - 1
         out = resid if last else fields.at[step + 1]
-        if step > 0:
+        if step > 0 and step in WHOLE:
             send_faces(now, step, step, 0)
 
         def finish(cell, delta, now=now, out=out, last=last):
@@ -341,6 +377,7 @@
 
         if step in PAIRED:
             inside(now, finish, functools.partial(send_edges, PAIRED.index(step), out))
+            send_edges_y(PAIRED.index(step), out)
         else:
             inside(now, finish)
             next_faces(step - 1)
@@ -380,10 +417,10 @@
     def _():
         sent_faces(fields.at[0], 0, 0, 0)
 
-    for step in range(1, STEPS):
+    for step in WHOLE[1:-1]:
         sent_faces(fields.at[step], step, step, 0)
     for pair in range(len(PAIRED)):
-        for f in range(2):
+        for f in range(4):
             pl.when(exists[f])(edge_copy(pair, f).wait_send)
 
     @pl.when(more)
@@ -437,9 +474,11 @@
                 pltpu.VMEM((STEPS + 1, 2, ny, 16, nz), F32),
                 pltpu.VMEM((STEPS + 1, 2, nx, 16, nz), F32),
                 pltpu.VMEM((STEPS + 2, 2, nx, 16, nz), F32),
-                pltpu.VMEM((STEPS // 2, 2, 2, 16, nz), F32),
+                pltpu.VMEM((2, STEPS // 2, 2, 2, 16, nz), F32),
                 pltpu.VMEM((STEPS // 2, 2, ny, 16, nz), F32),
                 pltpu.VMEM((STEPS // 2, 2, ny, 16, nz), F32),
+                pltpu.VMEM((STEPS // 2, 2, nx, 16, nz), F32),
+                pltpu.VMEM((STEPS // 2, 2, nx, 16, nz), F32),
                 stack, stack,
                 pltpu.SemaphoreType.DMA((5,)),
                 pltpu.SemaphoreType.DMA((STEPS + 2, 4)),
@@ -448,10 +487,10 @@
                 pltpu.SemaphoreType.DMA((nx,)),
                 pltpu.SemaphoreType.DMA((nx,)),
                 pltpu.SemaphoreType.DMA((nx,)),
-                pltpu.SemaphoreType.DMA((STEPS + 2, 4)),
+                pltpu.SemaphoreType.DMA((2, STEPS + 2, 4)),
+                pltpu.SemaphoreType.DMA((2, STEPS // 2, 4)),
                 pltpu.SemaphoreType.DMA((STEPS // 2, 4)),
-                pltpu.SemaphoreType.DMA((STEPS // 2, 2)),
-                pltpu.SemaphoreType.DMA((STEPS // 2, 2)),
+                pltpu.SemaphoreType.DMA((STEPS // 2, 4)),
             ],
             compiler_params=pltpu.CompilerParams(
                 collective_id=0, has_side_effects=True, vmem_limit_bytes=32 * 2**20

time: 26.2 us -> 25.1 us (0.958)
  Pallas kernels: 25.4 us -> 24.3 us
    pallas_call x1, Pallas kernels: 24.3 us -> 23.2 us  [local(): pl.pallas_call(functools.partial(kernel, counts, nx, ny), out_shape=(shap...]
where the time goes in v8:
time: 25.1 us; the launch traced here: 24.9 us
  Pallas kernels  24.3 us (97%)
  between operations  0.64 us (3%)
    pallas_call x1, Pallas kernels, local(): pl.pallas_call(functools.partial(kernel, counts, nx, ny), out_shape=(shap...  23.2 us
    pallas_call x1, Pallas kernels, local(): pl.pallas_call(functools.partial(finishing, nx, ny), out_shape=(flat,) *...  1.08 us

profile of v8, /device:TPU:1, one launch (start us, length us, event | category | flops | bytes accessed | tf_op | source)
XLA Modules:
  0.0 24.9 jit_solution(12465067453811528499)
XLA Ops:
  0.6 23.2 %cycle.1 = (f32[16,64,128]{2,1,0:T(8,128)S(1)}, f32[16,64,128]{2,1,0:T(8,128)S(1)}, f32[16,64,128]{2,1,0:T(8,128)S(1)}) custom-call(f32[1024,128]{1,0:T(8,128)} %bitcast.6, f32[1024,128]{1,0:T(8,128)} %bitcast.7, f32[1024,128]{1,0:T(8,128)} %bitcast.8, f32[64,64]{1,0:T(8,128)} %vol_hbm.1, f32[6,16,64]{2,1,0:T(8,128)} %bitcast.9), custom_call_target="tpu_custom_call" | custom-call | tf_op jit(solution)/shard_map/cycle/pallas_call | solution.py:466
  23.8 1.1 %finishing.1 = (f32[1024,128]{1,0:T(8,128)}, f32[1024,128]{1,0:T(8,128)}) custom-call(f32[16,64,128]{2,1,0:T(8,128)S(1)} %get-tuple-element.7.kept, f32[16,64,128]{2,1,0:T(8,128)S(1)} %get-tuple-element.8.resid, f32[16,64,128]{2,1,0:T(8,128)S(1)} %get-tuple-element.9.error), custom_call_target="tpu_custom_call" | custom-call | tf_op jit(solution)/shard_map/finishing/pallas_call | solution.py:508

commit v9 on v7

--- a/solution.py
+++ b/solution.py
@@ -96,11 +96,6 @@
             send_sem=start_send.at[x], recv_sem=start_recv.at[x],
             device_id={"tm": tm + 1, "sx": sx, "sy": sy}, device_id_type=MESH,
         )
-
-    @pl.when(more)
-    def _():
-        for x in range(nx):
-            start_copy(x).start()
 
     top = lax.broadcasted_iota(jnp.int32, (8, LANES), 0) < 4
     lane = lax.broadcasted_iota(jnp.int32, (16, LANES), 1)
@@ -218,6 +213,11 @@
         load_init.wait()
         reorder(raw_start, fields.at[0])
         send_faces(fields.at[0], 0, 0, 0)
+
+    @pl.when(more)
+    def _():
+        for x in range(nx):
+            start_copy(x).start()
 
     load_state.wait()
     reorder(raw_state, kept)

time: 24.2 us -> 24.2 us (level)
  no operation moved by 1% of the time
where the time goes in v9:
time: 24.2 us; the launch traced here: 24.1 us
  Pallas kernels  23.4 us (97%)
  between operations  0.64 us (3%)
    pallas_call x1, Pallas kernels, local(): pl.pallas_call(functools.partial(kernel, counts, nx, ny), out_shape=(shap...  22.3 us
    pallas_call x1, Pallas kernels, local(): pl.pallas_call(functools.partial(finishing, nx, ny), out_shape=(flat,) *...  1.08 us

profile of v9, /device:TPU:1, one launch (start us, length us, event | category | flops | bytes accessed | tf_op | source)
XLA Modules:
  0.0 24.1 jit_solution(15970845715910207947)
XLA Ops:
  0.6 22.3 %cycle.1 = (f32[16,64,128]{2,1,0:T(8,128)S(1)}, f32[16,64,128]{2,1,0:T(8,128)S(1)}, f32[16,64,128]{2,1,0:T(8,128)S(1)}) custom-call(f32[1024,128]{1,0:T(8,128)} %bitcast.6, f32[1024,128]{1,0:T(8,128)} %bitcast.7, f32[1024,128]{1,0:T(8,128)} %bitcast.8, f32[64,64]{1,0:T(8,128)} %vol_hbm.1, f32[6,16,64]{2,1,0:T(8,128)} %bitcast.9), custom_call_target="tpu_custom_call" | custom-call | tf_op jit(solution)/shard_map/cycle/pallas_call | solution.py:373
  23.0 1.1 %finishing.1 = (f32[1024,128]{1,0:T(8,128)}, f32[1024,128]{1,0:T(8,128)}) custom-call(f32[16,64,128]{2,1,0:T(8,128)S(1)} %get-tuple-element.7.kept, f32[16,64,128]{2,1,0:T(8,128)S(1)} %get-tuple-element.8.resid, f32[16,64,128]{2,1,0:T(8,128)S(1)} %get-tuple-element.9.error), custom_call_target="tpu_custom_call" | custom-call | tf_op jit(solution)/shard_map/finishing/pallas_call | solution.py:406
